TPU v7x, 512 devices: a whole 4x4x16 slice. The times are simulated.
512 devices in a mesh: shot: 16 (over x, z_hi), head: 32 (over z_lo, y, core).
Axes of the slice: x: 4, y: 4, z: 16 (z_hi: 4, z_lo: 4; z = z_hi * 4 + z_lo), core: 2. Of those that a mesh axis runs over, the one named last changes fastest.
Arguments:
- queries: bfloat16 [16, 2048, 4096], P('shot', 'head'), may hold values from -22 to 22
- key_rows: bfloat16 [16, 2048, 4096], P('shot', 'head'), may hold values from -4 to 4
- value_rows: bfloat16 [16, 2048, 4096], P('shot', 'head'), may hold values from -5 to 5
- shot_lengths: int32 [16], replicated, may hold values from 1024 to 2048, as said below
- shot_links: int32 [2, 16], replicated, may hold values 0 or 1
- block_select: int32 [2, 16, 2], replicated, may hold values from 0 to 15, as said below
Outputs:
- attended: bfloat16 [16, 2048, 4096], P('shot', 'head')
Inputs may be any that keep to these rules, and one draw needn't show every extreme that they name: `shot_lengths`: multiples of 128; some shot has exactly 2048 tokens and some exactly 1024. `block_select`: the 2 blocks of one [r, s] are different and lie wholly below the length of shot s XOR (16 >> (r + 1)).
All inputs are finite; a program needn't handle non-finite values.
Results may differ from a plain program's by a relative error of at most 0.0047.
Values may be sent and summed in bfloat16 or wider, within the bound.
No kernel may reach another device: no remote copies, remote signals or barrier semaphores. Data moves between devices by JAX's collectives and lax.ppermute only.
A program may use at most 64 MiB of HBM per device.

v0:
```python
import jax
import jax.numpy as jnp
from jax import lax
from jax.sharding import PartitionSpec as P

HEAD_DIM = 128
LMAX = 2048
BLK = 128
SEL = 2
ROUNDS = 2


def from_partner(block, axis, bit):
    count = lax.axis_size(axis)
    route = []
    for low in range(count):
        high = low | 1 << bit
        if high != low and high < count:
            route += [(low, high), (high, low)]
    return lax.ppermute(block, axis, route)


def take_blocks(source, chosen):
    feature_width = source.shape[1]
    shaped = source.reshape(source.shape[0] // BLK, BLK, feature_width)
    return shaped[chosen].reshape(chosen.shape[0] * BLK, feature_width)


def attend(query_rows, key_all, value_all, key_bias):
    length = query_rows.shape[0]
    feature_width = query_rows.shape[1]
    head_count = feature_width // HEAD_DIM
    query_heads = query_rows.reshape(length, head_count, HEAD_DIM)
    key_heads = key_all.reshape(-1, head_count, HEAD_DIM)
    value_heads = value_all.reshape(-1, head_count, HEAD_DIM)
    block_rows = min(512, length)
    scale = HEAD_DIM ** (-0.5)

    def block_attend(query_block):
        scores = (
            jnp.einsum("qhd,khd->hqk", query_block, key_heads, preferred_element_type=jnp.float32)
            * scale
            + key_bias
        )
        row_max = jnp.max(scores, axis=2, keepdims=True)
        exp_terms = jnp.exp(scores - row_max)
        denominator = jnp.sum(exp_terms, axis=2)
        weights = exp_terms.astype(jnp.bfloat16)
        weighted = jnp.einsum(
            "hqk,khd->qhd", weights, value_heads, preferred_element_type=jnp.float32
        )
        return weighted / jnp.transpose(denominator)[:, :, None]

    blocks = query_heads.reshape(length // block_rows, block_rows, head_count, HEAD_DIM)
    return lax.map(block_attend, blocks).reshape(length, feature_width)


def partner_rows(key_local, value_local, shot_links, block_select, shot_index, levels):
    far_count = SEL * BLK
    key_parts = []
    value_parts = []
    bias_parts = []
    for round_index in range(ROUNDS):
        bit_number = levels - 1 - round_index
        key_far, value_far = from_partner((key_local, value_local), "shot", bit_number)
        chosen = block_select[round_index, shot_index]
        key_part = take_blocks(key_far, chosen)
        value_part = take_blocks(value_far, chosen)
        key_parts.append(key_part)
        value_parts.append(value_part)
        linked = shot_links[round_index, shot_index]
        bias_parts.append(
            jnp.where(
                linked > 0,
                jnp.zeros((far_count,), jnp.float32),
                jnp.full((far_count,), -1e30, jnp.float32),
            )
        )
    return (key_parts, value_parts, bias_parts)


def body(queries, key_rows, value_rows, shot_lengths, shot_links, block_select):
    shot_index = lax.axis_index("shot")
    levels = lax.axis_size("shot").bit_length() - 1
    query_local, key_local, value_local = (
        lax.all_to_all(queries, "head", split_axis=2, concat_axis=1, tiled=True),
        lax.all_to_all(key_rows, "head", split_axis=2, concat_axis=1, tiled=True),
        lax.all_to_all(value_rows, "head", split_axis=2, concat_axis=1, tiled=True),
    )
    key_parts, value_parts, bias_parts = partner_rows(
        key_local[0], value_local[0], shot_links, block_select, shot_index, levels
    )
    positions = jnp.arange(LMAX, dtype=jnp.int32)
    own_length = shot_lengths[shot_index]
    own_bias = jnp.where(
        positions < own_length,
        jnp.zeros((LMAX,), jnp.float32),
        jnp.full((LMAX,), -1e30, jnp.float32),
    )
    key_all = jnp.concatenate([key_local[0]] + key_parts, axis=0)
    value_all = jnp.concatenate([value_local[0]] + value_parts, axis=0)
    key_bias = jnp.concatenate([own_bias] + bias_parts, axis=0)
    result = attend(query_local[0], key_all, value_all, key_bias)
    live = (positions < own_length)[:, None]
    output = jnp.where(live, result, jnp.zeros_like(result)).astype(jnp.bfloat16)
    return lax.all_to_all(output[None], "head", split_axis=1, concat_axis=2, tiled=True)


def solution(mesh):
    placed = (
        P("shot", "head", None),
        P("shot", "head", None),
        P("shot", "head", None),
        P(),
        P(),
        P(),
    )
    return jax.shard_map(
        body, mesh=mesh, in_specs=placed, out_specs=P("shot", "head", None), check_vma=False
    )
```

profile of v0, /device:TPU:1, one launch (start us, length us, event | category | flops | bytes accessed | tf_op | source)
XLA Modules:
  0.0 230.6 jit_solution(1441018019651595748)
XLA Ops:
  0.0 4.9 %copy.39 = bf16[1,64,4096]{1,0,2:T(2,128)(2,1)S(1)} copy(bf16[1,64,4096]{2,1,0:T(8,128)(2,1)} %param.9) | data formatting | bytes 1048576 | tf_op args[1]
  5.4 22.3 %reduce.9 = bf16[4096,64]{1,0:T(8,128)(2,1)S(1)} reduce(bf16[4096,1,64]{2,1,0:T(2,128)(2,1)S(1)} %bitcast.111, bf16[]{:T(256)} %broadcast.107), dimensions={1}, to_apply=%bitcast.83.reduce_sub_computation | reduce | bytes 1048578
  27.7 1.5 reshape.217
  29.2 11.1 %all-to-all-start.1 = ((bf16[32,2,4096]{2,1,0:T(2,128)(2,1)}), bf16[32,2,4096]{2,1,0:T(2,128)(2,1)}, u32[]{:S(2)}, u32[]{:S(2)}) async-start(bf16[32,2,4096]{2,1,0:T(2,128)(2,1)} %reshape.217), calls=%async_computation.1 | async-start | bytes 1048576 | tf_op jit(solution)/shard_map/all_to_all | solution.py:87
  40.3 4.9 %copy.42 = bf16[1,64,4096]{1,0,2:T(2,128)(2,1)S(1)} copy(bf16[1,64,4096]{2,1,0:T(8,128)(2,1)} %param.10) | data formatting | bytes 1048576 | tf_op args[2]
  45.2 22.3 %reduce.10 = bf16[4096,64]{1,0:T(8,128)(2,1)S(1)} reduce(bf16[4096,1,64]{2,1,0:T(2,128)(2,1)S(1)} %bitcast.112, bf16[]{:T(256)} %broadcast.107), dimensions={1}, to_apply=%bitcast.85.reduce_sub_computation | reduce | bytes 1048578
  67.6 1.6 reshape.219
  69.1 7.9 %all-to-all-start.2 = ((bf16[32,2,4096]{2,1,0:T(2,128)(2,1)}), bf16[32,2,4096]{2,1,0:T(2,128)(2,1)}, u32[]{:S(2)}, u32[]{:S(2)}) async-start(bf16[32,2,4096]{2,1,0:T(2,128)(2,1)} %reshape.219), calls=%async_computation.2 | async-start | bytes 1048576 | tf_op jit(solution)/shard_map/all_to_all | solution.py:88
  77.0 4.9 %copy.36 = bf16[1,64,4096]{1,0,2:T(2,128)(2,1)S(1)} copy(bf16[1,64,4096]{2,1,0:T(8,128)(2,1)} %param.8) | data formatting | bytes 1048576 | tf_op args[0]
  81.9 22.3 %reduce.8 = bf16[4096,64]{1,0:T(8,128)(2,1)S(1)} reduce(bf16[4096,1,64]{2,1,0:T(2,128)(2,1)S(1)} %bitcast.113, bf16[]{:T(256)} %broadcast.107), dimensions={1}, to_apply=%bitcast.81.reduce_sub_computation | reduce | bytes 1048578
  104.3 1.5 reshape.215
  105.8 7.7 %all-to-all-start = ((bf16[32,2,4096]{2,1,0:T(2,128)(2,1)}), bf16[32,2,4096]{2,1,0:T(2,128)(2,1)S(1)}, u32[]{:S(2)}, u32[]{:S(2)}) async-start(bf16[32,2,4096]{2,1,0:T(2,128)(2,1)} %reshape.215), calls=%async_computation | async-start | bytes 1048576 | tf_op jit(solution)/shard_map/all_to_all | solution.py:86
  114.5 4.1 %reshape.218 = bf16[4096,1,64]{2,1,0:T(2,128)(2,1)S(1)} reshape(bf16[32,2,4096]{2,1,0:T(2,128)(2,1)} %all-to-all-done.1) | data formatting | bytes 1048576
  118.6 2.3 copy.40
  121.3 3.7 %collective-permute-start = (bf16[2048,128]{1,0:T(8,128)(2,1)S(1)}, bf16[2048,128]{1,0:T(8,128)(2,1)}, u32[]{:S(2)}, u32[]{:S(2)}) collective-permute-start(bf16[2048,128]{1,0:T(8,128)(2,1)S(1)} %bitcast.116), channel_id=1, source_target_pairs={{0,256},{256,0},{32,288},{288,32},{64,320},{320,64},{96,352},{352,... | collective-permute-start | bytes 1572872 | tf_op jit(solution)/shard_map/ppermute | solution.py:20
  125.0 2.2 collective-permute-start.1
  127.2 4.1 %reshape.220 = bf16[4096,1,64]{2,1,0:T(2,128)(2,1)S(1)} reshape(bf16[32,2,4096]{2,1,0:T(2,128)(2,1)} %all-to-all-done.2) | data formatting | bytes 1048576
  131.4 3.6 %copy.43 = bf16[1,64,4096]{2,1,0:T(8,128)(2,1)} copy(bf16[1,64,4096]{1,0,2:T(2,128)(2,1)S(1)} %bitcast.109) | data formatting | bytes 1048576 | tf_op jit(solution)/shard_map/all_to_all | solution.py:88
  137.2 3.6 %collective-permute-start.2 = (bf16[2048,128]{1,0:T(8,128)(2,1)}, bf16[2048,128]{1,0:T(8,128)(2,1)}, u32[]{:S(2)}, u32[]{:S(2)}) collective-permute-start(bf16[2048,128]{1,0:T(8,128)(2,1)} %bitcast.23), channel_id=1, source_target_pairs={{0,256},{256,0},{32,288},{288,32},{64,320},{320,64},{96,352},{352,... | collective-permute-start | bytes 1572872 | tf_op jit(solution)/shard_map/ppermute | solution.py:20
  140.8 2.2 collective-permute-start.3
  146.3 1.2 reshape.216
  147.6 2.3 copy.37
  150.2 1.6 gather_fusion
  151.9 8.7 %collective-permute-done.2 = bf16[2048,128]{1,0:T(8,128)(2,1)} collective-permute-done((bf16[2048,128]{1,0:T(8,128)(2,1)}, bf16[2048,128]{1,0:T(8,128)(2,1)}, u32[]{:S(2)}, u32[]{:S(2)}) %collective-permute-start.2) | collective-permute-done | bytes 524320 | tf_op jit(solution)/shard_map/ppermute | solution.py:20
  160.5 1.6 gather_fusion.2
  162.2 2.2 gather_fusion.1
  164.4 6.5 %collective-permute-done.3 = bf16[2048,128]{1,0:T(8,128)(2,1)} collective-permute-done((bf16[2048,128]{1,0:T(8,128)(2,1)}, bf16[2048,128]{1,0:T(8,128)(2,1)}, u32[]{:S(2)}, u32[]{:S(2)}) %collective-permute-start.3) | collective-permute-done | bytes 524320 | tf_op jit(solution)/shard_map/ppermute | solution.py:20
  170.9 2.2 gather_fusion.3
  174.3 11.0 %while.10 = (s32[]{:T(128)}, f32[4,512,1,128]{3,1,2,0:T(8,128)S(1)}, bf16[4,512,1,128]{3,1,2,0:T(8,128)(2,1)S(1)}, bf16[2560,1,128]{2,0,1:T(8,128)(2,1)S(1)}, f3...) while((s32[]{:T(128)}, f32[4,512,1,128]{3,1,2,0:T(8,128)S(1)}, ...), condition=%wide.region_3.4_spmd, body=%wide.region_0.3_spmd.sunk | while | flops 680328192 | bytes 17455188 | solution.py:55
  185.4 7.5 %fusion.26 = bf16[2048,1,128]{2,1,0:T(2,128)(2,1)S(1)} fusion(f32[1,2048,128]{2,0,1:T(1,128)S(1)} %bitcast.126, pred[2048]{0:T(1024)(128)(4,1)S(1)} %iota_compare_fusion), kind=kLoop, calls=%fused_computation.41 | loop fusion | flops 262144 | bytes 1574912
  192.9 11.4 %reduce.11 = bf16[2048,128]{1,0:T(8,128)(2,1)S(1)} reduce(bf16[2048,1,128]{2,1,0:T(2,128)(2,1)S(1)} %fusion.26, bf16[]{:T(256)} %broadcast.107), dimensions={1}, to_apply=%fusion.26.reduce_sub_computation | reduce | bytes 1048578
  204.4 24.6 %all_to_all.63 = bf16[32,2,4096]{2,1,0:T(2,128)(2,1)S(1)} all-to-all(bf16[32,2,4096]{2,1,0:T(2,128)(2,1)S(1)} %reshape.221), channel_id=1, replica_groups=mesh['shot'=16,'head'=32] {'head'}, dimensions={0} | all-to-all | bytes 1048576 | tf_op jit(solution)/shard_map/all_to_all | solution.py:106
  (53 shorter events, 20.0 us)
Async XLA Ops:
  29.2 39.9 %all-to-all-start.1 = ((bf16[32,2,4096]{2,1,0:T(2,128)(2,1)}), bf16[32,2,4096]{2,1,0:T(2,128)(2,1)}, u32[]{:S(2)}, u32[]{:S(2)}) async-start(bf16[32,2,4096]{2,1,0:T(2,128)(2,1)} %reshape.217), calls=%async_computation.1 | async-start | bytes 1048576 | tf_op jit(solution)/shard_map/all_to_all | solution.py:87
  69.1 36.7 %all-to-all-start.2 = ((bf16[32,2,4096]{2,1,0:T(2,128)(2,1)}), bf16[32,2,4096]{2,1,0:T(2,128)(2,1)}, u32[]{:S(2)}, u32[]{:S(2)}) async-start(bf16[32,2,4096]{2,1,0:T(2,128)(2,1)} %reshape.219), calls=%async_computation.2 | async-start | bytes 1048576 | tf_op jit(solution)/shard_map/all_to_all | solution.py:88
  81.9 31.6 %copy-start.3 = (s32[16]{0:T(128)S(1)}, s32[16]{0:T(128)}, u32[]{:S(2)}) copy-start(s32[16]{0:T(128)} %param.11) | copy-start | bytes 196
  81.9 32.3 %copy-start.1 = (s32[2,16,2]{1,2,0:T(2,128)S(1)}, s32[2,16,2]{1,2,0:T(2,128)}, u32[]{:S(2)}) copy-start(s32[2,16,2]{1,2,0:T(2,128)} %param.13) | copy-start | bytes 772
  105.8 40.5 %all-to-all-start = ((bf16[32,2,4096]{2,1,0:T(2,128)(2,1)}), bf16[32,2,4096]{2,1,0:T(2,128)(2,1)S(1)}, u32[]{:S(2)}, u32[]{:S(2)}) async-start(bf16[32,2,4096]{2,1,0:T(2,128)(2,1)} %reshape.215), calls=%async_computation | async-start | bytes 1048576 | tf_op jit(solution)/shard_map/all_to_all | solution.py:86
  121.3 28.9 %collective-permute-start = (bf16[2048,128]{1,0:T(8,128)(2,1)S(1)}, bf16[2048,128]{1,0:T(8,128)(2,1)}, u32[]{:S(2)}, u32[]{:S(2)}) collective-permute-start(bf16[2048,128]{1,0:T(8,128)(2,1)S(1)} %bitcast.116), channel_id=1, source_target_pairs={{0,256},{256,0},{32,288},{288,32},{64,320},{320,64},{96,352},{352,... | collective-permute-start | bytes 1572872 | tf_op jit(solution)/shard_map/ppermute | solution.py:20
  125.0 37.2 %collective-permute-start.1 = (bf16[2048,128]{1,0:T(8,128)(2,1)S(1)}, bf16[2048,128]{1,0:T(8,128)(2,1)}, u32[]{:S(2)}, u32[]{:S(2)}) collective-permute-start(bf16[2048,128]{1,0:T(8,128)(2,1)S(1)} %bitcast.117), channel_id=1, source_target_pairs={{0,128},{128,0},{32,160},{160,32},{64,192},{192,64},{96,224},{224,... | collective-permute-start | bytes 1572872 | tf_op jit(solution)/shard_map/ppermute | solution.py:20
  131.4 12.3 %copy-start.2 = (s32[2,16]{1,0:T(2,128)S(1)}, s32[2,16]{1,0:T(2,128)}, u32[]{:S(2)}) copy-start(s32[2,16]{1,0:T(2,128)} %param.12) | copy-start | bytes 388
  137.2 23.3 %collective-permute-start.2 = (bf16[2048,128]{1,0:T(8,128)(2,1)}, bf16[2048,128]{1,0:T(8,128)(2,1)}, u32[]{:S(2)}, u32[]{:S(2)}) collective-permute-start(bf16[2048,128]{1,0:T(8,128)(2,1)} %bitcast.23), channel_id=1, source_target_pairs={{0,256},{256,0},{32,288},{288,32},{64,320},{320,64},{96,352},{352,... | collective-permute-start | bytes 1572872 | tf_op jit(solution)/shard_map/ppermute | solution.py:20
  140.8 30.1 %collective-permute-start.3 = (bf16[2048,128]{1,0:T(8,128)(2,1)}, bf16[2048,128]{1,0:T(8,128)(2,1)}, u32[]{:S(2)}, u32[]{:S(2)}) collective-permute-start(bf16[2048,128]{1,0:T(8,128)(2,1)} %bitcast.23), channel_id=1, source_target_pairs={{0,128},{128,0},{32,160},{160,32},{64,192},{192,64},{96,224},{224,... | collective-permute-start | bytes 1572872 | tf_op jit(solution)/shard_map/ppermute | solution.py:20
  149.9 24.4 %copy-start = (f32[4,512,1,128]{3,1,2,0:T(8,128)S(1)}, f32[4,512,1,128]{3,1,2,0:T(8,128)}, u32[]{:S(2)}) copy-start(f32[4,512,1,128]{3,1,2,0:T(8,128)} %custom-call.8) | copy-start | bytes 3145732
where the time goes:
time: 232 us; the launch traced here: 231 us
  other arithmetic  91.8 us (40%)
  local copies, waits for them, and re-layouts  51.1 us (22%)
  starting transfers between devices  38.5 us (17%)
  blocking collectives  24.6 us (11%)
  waiting for transfers between devices  15.2 us (7%)
  matrix products  7.59 us (3%)
    unnamed x5, other arithmetic  85.9 us
    unnamed x24, local copies, waits for them, and re-layouts  31.3 us
    all_to_all x1, blocking collectives, body(): lax.all_to_all(output[None], 'head', split_axis=1, concat_axis=2, tiled=T...  24.6 us
    ppermute x4, waiting for transfers between devices, from_partner(): return lax.ppermute(block, axis, route)  15.2 us
    ppermute x4, starting transfers between devices, from_partner(): return lax.ppermute(block, axis, route)  11.7 us
    all_to_all x1, starting transfers between devices, body(): lax.all_to_all(key_rows, 'head', split_axis=2, concat_axis=1, tiled=True)  11.1 us
    all_to_all x1, starting transfers between devices, body(): lax.all_to_all(value_rows, 'head', split_axis=2, concat_axis=1, tiled=True)  7.91 us
    all_to_all x1, starting transfers between devices, body(): lax.all_to_all(queries, 'head', split_axis=2, concat_axis=1, tiled=True)  7.73 us
  transfers between devices with their start and end apart: 7, of which 2 were waited for; matrix products, arithmetic and copies ran while one was open for 37% of the time, Pallas kernels for 0%

commit v1 on v0

v1 whole, which is shorter than its diff:
```python
import jax
import jax.numpy as jnp
from jax import lax
from jax.experimental import pallas as pl
from jax.experimental.pallas import tpu as pltpu
from jax.sharding import PartitionSpec as P

HEAD_DIM = 128
LMAX = 2048
LMIN = 1024
BLK = 128
SEL = 2
ROUNDS = 2
SHOTS = 16
FAR = SEL * BLK
SCALE = HEAD_DIM ** (-0.5)
LOG2E = 1.4426950408889634
NEG = -1e30
CHUNK = 256
SUB = 256
VMEM_BYTES = 24 << 20
SMALL_BYTES = 6 << 20


def split_heads_kernel(*refs):
    *sources, out_ref = refs
    heads, _, _ = out_ref.shape
    rows = sources[0].shape[0]
    for number, source in enumerate(sources):
        for head in range(heads):
            out_ref[head, number * rows : (number + 1) * rows, :] = source[
                :, head * HEAD_DIM : (head + 1) * HEAD_DIM
            ]


def split_heads(*arrays):
    rows, width = arrays[0].shape
    heads = width // HEAD_DIM
    return pl.pallas_call(
        split_heads_kernel,
        in_specs=[pl.BlockSpec(memory_space=pltpu.VMEM)] * len(arrays),
        out_specs=pl.BlockSpec(memory_space=pltpu.VMEM),
        out_shape=jax.ShapeDtypeStruct((heads, len(arrays) * rows, HEAD_DIM), jnp.bfloat16),
        compiler_params=pltpu.CompilerParams(vmem_limit_bytes=SMALL_BYTES),
        name="split_heads",
    )(*arrays)


def join_heads_kernel(source, out_ref):
    heads, _, _ = source.shape
    for head in range(heads):
        out_ref[:, head * HEAD_DIM : (head + 1) * HEAD_DIM] = source[head]


def join_heads(array):
    heads, rows, _ = array.shape
    return pl.pallas_call(
        join_heads_kernel,
        in_specs=[pl.BlockSpec(memory_space=pltpu.VMEM)],
        out_specs=pl.BlockSpec(memory_space=pltpu.VMEM),
        out_shape=jax.ShapeDtypeStruct((rows, heads * HEAD_DIM), jnp.bfloat16),
        compiler_params=pltpu.CompilerParams(vmem_limit_bytes=SMALL_BYTES),
        name="join_heads",
    )(array)


def pick_kernel(block_select, own_ref, *outs):
    shot = lax.axis_index("shot")
    piece = own_ref.shape[1] // 2
    group = BLK // piece
    for round_index, out_ref in enumerate(outs):
        partner = shot ^ (SHOTS >> (round_index + 1))
        for pick in range(SEL):
            first = block_select[round_index, partner, pick] * group
            out_ref[pick * group : (pick + 1) * group] = own_ref[pl.ds(first, group)]


def pick_blocks(block_select, own):
    shape = jax.ShapeDtypeStruct((FAR // (own.shape[1] // 2),) + own.shape[1:], jnp.bfloat16)
    return pl.pallas_call(
        pick_kernel,
        in_specs=[
            pl.BlockSpec(memory_space=pltpu.SMEM),
            pl.BlockSpec(memory_space=pltpu.VMEM),
        ],
        out_specs=[pl.BlockSpec(memory_space=pltpu.VMEM)] * ROUNDS,
        out_shape=[shape] * ROUNDS,
        compiler_params=pltpu.CompilerParams(vmem_limit_bytes=SMALL_BYTES),
        name="pick_blocks",
    )(block_select, own)


def attend_kernel(lengths, links, query_ref, own_ref, *refs):
    *far_refs, out_ref, value_ref = refs
    shot = lax.axis_index("shot")
    length = lengths[shot]
    piece = query_ref.shape[1]
    group = CHUNK // piece
    lane = lax.broadcasted_iota(jnp.int32, (1, CHUNK), 1)
    keys, bias = [], []

    def add_keys(source, first, shift):
        place = slice(first, first + group)
        spot = slice(len(keys) * CHUNK, (len(keys) + 1) * CHUNK)
        keys.append(source[place, 0:piece, :].reshape(CHUNK, HEAD_DIM))
        value_ref[spot, :HEAD_DIM] = source[place, piece : 2 * piece, :].reshape(CHUNK, HEAD_DIM)
        value_ref[spot, HEAD_DIM:] = jnp.ones((CHUNK, HEAD_DIM), jnp.bfloat16)
        bias.append(shift)

    for chunk in range(LMAX // CHUNK):
        shift = None
        if (chunk + 1) * CHUNK > LMIN:
            shift = jnp.where(lane + chunk * CHUNK < length, 0.0, NEG).astype(jnp.float32)
        add_keys(own_ref, chunk * group, shift)
    for round_index, far_ref in enumerate(far_refs):
        shift = jnp.where(links[round_index, shot] > 0, 0.0, NEG).astype(jnp.float32)
        for chunk in range(FAR // CHUNK):
            add_keys(far_ref, chunk * group, shift)

    parts = LMAX // SUB
    scores, row_max = None, None
    for part in range(parts + 1):
        new_scores, top, weighted = [], None, None
        if part < parts:
            place = slice(part * SUB // piece, (part + 1) * SUB // piece)
            query = query_ref[place].reshape(SUB, HEAD_DIM)
        for chunk, (key, shift) in enumerate(zip(keys, bias)):
            if part < parts:
                score = lax.dot_general(
                    query, key, (((1,), (1,)), ((), ())), preferred_element_type=jnp.float32
                )
                if shift is not None:
                    score = score + shift
                new_scores.append(score)
                top = score if top is None else jnp.maximum(top, score)
            if part > 0:
                terms = jnp.exp2(scores[chunk] * (SCALE * LOG2E) - row_max)
                product = jnp.dot(
                    terms.astype(jnp.bfloat16),
                    value_ref[chunk * CHUNK : (chunk + 1) * CHUNK, :],
                    preferred_element_type=jnp.float32,
                )
                weighted = product if weighted is None else weighted + product
        if part > 0:
            first = (part - 1) * SUB
            position = first + lax.broadcasted_iota(jnp.int32, (SUB, 1), 0)
            result = weighted[:, :HEAD_DIM] / weighted[:, HEAD_DIM : HEAD_DIM + 1]
            result = jnp.where(position < length, result, 0.0).astype(jnp.bfloat16)
            out_ref[first // piece : (first + SUB) // piece] = result.reshape(
                SUB // piece, piece, HEAD_DIM
            )
        if part < parts:
            scores, row_max = new_scores, jnp.max(top, axis=1, keepdims=True) * (SCALE * LOG2E)


def attend(lengths, links, query, own, *far):
    keys = LMAX + ROUNDS * FAR
    smem = pl.BlockSpec(memory_space=pltpu.SMEM)
    vmem = pl.BlockSpec(memory_space=pltpu.VMEM)
    return pl.pallas_call(
        attend_kernel,
        in_specs=[smem, smem] + [vmem] * (2 + ROUNDS),
        out_specs=vmem,
        out_shape=jax.ShapeDtypeStruct(query.shape, jnp.bfloat16),
        scratch_shapes=[pltpu.VMEM((keys, 2 * HEAD_DIM), jnp.bfloat16)],
        compiler_params=pltpu.CompilerParams(vmem_limit_bytes=VMEM_BYTES),
        cost_estimate=pl.CostEstimate(
            flops=4 * LMAX * keys * HEAD_DIM, bytes_accessed=2 << 20, transcendentals=LMAX * keys
        ),
        name="attend",
    )(lengths, links, query, own, *far)


def swap(array):
    return lax.all_to_all(array, "head", split_axis=0, concat_axis=0, tiled=True)


def from_partner(array, bit):
    count = lax.axis_size("shot")
    return lax.ppermute(array, "shot", [(low, low ^ bit) for low in range(count)])


def body(queries, key_rows, value_rows, shot_lengths, shot_links, block_select):
    own = swap(split_heads(key_rows[0], value_rows[0]))
    query = swap(split_heads(queries[0]))
    far = [
        from_partner(picked, SHOTS >> (round_index + 1))
        for round_index, picked in enumerate(pick_blocks(block_select, own))
    ]
    result = attend(shot_lengths, shot_links, query, own, *far)
    return join_heads(swap(result))[None]


def solution(mesh):
    placed = (
        P("shot", "head", None),
        P("shot", "head", None),
        P("shot", "head", None),
        P(),
        P(),
        P(),
    )
    return jax.shard_map(
        body, mesh=mesh, in_specs=placed, out_specs=P("shot", "head", None), check_vma=False
    )
```

time: 232 us -> 91.4 us (0.39)
  other arithmetic: 91.8 us -> 0 us
  local copies, waits for them, and re-layouts: 51.1 us -> 2.19 us
  waiting for transfers between devices: 15.2 us -> 34.6 us
  starting transfers between devices: 38.5 us -> 22.3 us
  Pallas kernels: 0 us -> 11.4 us
  matrix products: 7.59 us -> 0 us
  blocking collectives: 24.6 us -> 20.3 us
    unnamed x5 -> x0, other arithmetic: 85.9 us -> none
    all_to_all x3 -> x2, waiting for transfers between devices: 0.01 us -> 34.6 us  [swap(): lax.all_to_all(array, 'head', split_axis=0, concat_axis=0, tiled=True)]
    unnamed x24 -> x13, local copies, waits for them, and re-layouts: 31.3 us -> 2.19 us
    ppermute x4 -> x2, waiting for transfers between devices: 15.2 us -> 0.01 us  [from_partner(): lax.ppermute(array, 'shot', [(low, low ^ bit) for low in range(count)])]
    pallas_call x0 -> x5, Pallas kernels: none -> 11.4 us  [the longest x1 7.6 us: attend(): pl.pallas_call(attend_kernel, in_specs=[smem, smem] + [vmem] * (2 + ROUND...]
    all_to_all x3 -> x2, starting transfers between devices: 26.7 us -> 15.7 us  [swap(): lax.all_to_all(array, 'head', split_axis=0, concat_axis=0, tiled=True)]
    all_to_all x10 -> x0, local copies, waits for them, and re-layouts: 10.6 us -> none  [the longest x3 4.67 us: body(): lax.all_to_all(value_rows, 'head', split_axis=2, concat_axis=1, tiled=True)]
    gather x4 -> x0, local copies, waits for them, and re-layouts: 7.69 us -> none  [take_blocks(): return shaped[chosen].reshape(chosen.shape[0] * BLK, feature_width)]
  transfers between devices with their start and end apart: 7 -> 4, of which waited for: 2 -> 2; matrix products, arithmetic and copies ran while one was open for 37% -> 0% of each run, Pallas kernels for 0% -> 2%
where the time goes in v1:
time: 91.4 us; the launch traced here: 90.9 us
  waiting for transfers between devices  34.6 us (38%)
  starting transfers between devices  22.3 us (24%)
  blocking collectives  20.3 us (22%)
  Pallas kernels  11.4 us (12%)
  local copies, waits for them, and re-layouts  2.19 us (2%)
    all_to_all x2, waiting for transfers between devices, swap(): lax.all_to_all(array, 'head', split_axis=0, concat_axis=0, tiled=True)  34.6 us
    all_to_all x1, blocking collectives, swap(): lax.all_to_all(array, 'head', split_axis=0, concat_axis=0, tiled=True)  20.3 us
    all_to_all x2, starting transfers between devices, swap(): lax.all_to_all(array, 'head', split_axis=0, concat_axis=0, tiled=True)  15.7 us
    pallas_call x1, Pallas kernels, attend(): pl.pallas_call(attend_kernel, in_specs=[smem, smem] + [vmem] * (2 + ROUND...  7.6 us
    ppermute x2, starting transfers between devices, from_partner(): lax.ppermute(array, 'shot', [(low, low ^ bit) for low in range(count)])  6.59 us
    unnamed x13, local copies, waits for them, and re-layouts  2.19 us
    pallas_call x2, Pallas kernels, split_heads(): pl.pallas_call(split_heads_kernel, in_specs=[pl.BlockSpec(memory_space=pl...  2.04 us
  transfers between devices with their start and end apart: 4, of which 2 were waited for; matrix products, arithmetic and copies ran while one was open for 0% of the time, Pallas kernels for 2%

profile of v1, /device:TPU:1, one launch (start us, length us, event | category | flops | bytes accessed | tf_op | source)
XLA Modules:
  0.0 90.9 jit_solution(15895610147687961046)
XLA Ops:
  0.0 0.0 copy-start.1
  0.0 1.0 %copy-done.1 = bf16[1,64,4096]{2,1,0:T(8,128)(2,1)S(1)} copy-done((bf16[1,64,4096]{2,1,0:T(8,128)(2,1)S(1)}, bf16[1,64,4096]{2,1,0:T(8,128)(2,1)}, u32[]{:S(2)}) %copy-start.1) | copy-done | bytes 524312
  1.0 0.0 copy-start.2
  1.0 1.0 %copy-done.2 = bf16[1,64,4096]{2,1,0:T(8,128)(2,1)S(1)} copy-done((bf16[1,64,4096]{2,1,0:T(8,128)(2,1)S(1)}, bf16[1,64,4096]{2,1,0:T(8,128)(2,1)}, u32[]{:S(2)}) %copy-start.2) | copy-done | bytes 524312
  2.1 1.2 %split_heads.3 = bf16[32,128,128]{2,1,0:T(8,128)(2,1)} custom-call(bf16[64,4096]{1,0:T(8,128)(2,1)S(1)} %bitcast.5, bf16[64,4096]{1,0:T(8,128)(2,1)S(1)} %bitcast.6), custom_call_target="tpu_custom_call" | custom-call | tf_op jit(solution)/shard_map/split_heads/pallas_call | solution.py:39
  3.2 0.0 copy-start
  3.2 10.6 %all-to-all-start.1 = ((bf16[32,128,128]{2,1,0:T(8,128)(2,1)}), bf16[32,128,128]{2,1,0:T(8,128)(2,1)S(1)}, u32[]{:S(2)}, u32[]{:S(2)}) async-start(bf16[32,128,128]{2,1,0:T(8,128)(2,1)} %split_heads.3), calls=%async_computation.1 | async-start | bytes 2097152 | tf_op jit(solution)/shard_map/all_to_all | solution.py:175
  13.8 0.0 copy-done
  13.9 0.9 split_heads.2
  14.7 0.0 copy-start.5
  14.7 25.8 %all-to-all-done.1.own_ref = bf16[32,128,128]{2,1,0:T(8,128)(2,1)S(1)} async-done(((bf16[32,128,128]{2,1,0:T(8,128)(2,1)}), bf16[32,128,128]{2,1,0:T(8,128)(2,1)S(1)}, u32[]{:S(2)}, u32[]{:S(2)}) %all-to-all-start.1) | async-done | bytes 1048608 | tf_op jit(solution)/shard_map/all_to_all | solution.py:175
  40.5 5.1 %all-to-all-start = ((bf16[32,64,128]{2,1,0:T(8,128)(2,1)}), bf16[32,64,128]{2,1,0:T(8,128)(2,1)S(1)}, u32[]{:S(2)}, u32[]{:S(2)}) async-start(bf16[32,64,128]{2,1,0:T(8,128)(2,1)} %split_heads.2), calls=%async_computation | async-start | bytes 1048576 | tf_op jit(solution)/shard_map/all_to_all | solution.py:175
  45.7 0.0 copy-done.5
  45.7 0.1 copy.7.block_select
  45.8 0.8 pick_blocks.1
  46.6 0.0 copy-start.3
  46.6 0.0 copy-start.4
  46.6 4.4 %collective-permute-start = (bf16[4,128,128]{2,1,0:T(8,128)(2,1)S(1)}, bf16[4,128,128]{2,1,0:T(8,128)(2,1)S(1)}, u32[]{:S(2)}, u32[]{:S(2)}) collective-permute-start(bf16[4,128,128]{2,1,0:T(8,128)(2,1)S(1)} %get-tuple-element.7), channel_id=1, source_target_pairs={{0,256},{32,288},{64,320},{96,352},{128,384},{160,416},{192,448},{... | collective-permute-start | bytes 393224 | tf_op jit(solution)/shard_map/ppermute | solution.py:180
  51.0 2.2 %collective-permute-start.1 = (bf16[4,128,128]{2,1,0:T(8,128)(2,1)S(1)}, bf16[4,128,128]{2,1,0:T(8,128)(2,1)S(1)}, u32[]{:S(2)}, u32[]{:S(2)}) collective-permute-start(bf16[4,128,128]{2,1,0:T(8,128)(2,1)S(1)} %get-tuple-element.8), channel_id=1, source_target_pairs={{0,128},{32,160},{64,192},{96,224},{128,0},{160,32},{192,64},{224,... | collective-permute-start | bytes 393224 | tf_op jit(solution)/shard_map/ppermute | solution.py:180
  53.2 8.8 %all-to-all-done.query_ref = bf16[32,64,128]{2,1,0:T(8,128)(2,1)S(1)} async-done(((bf16[32,64,128]{2,1,0:T(8,128)(2,1)}), bf16[32,64,128]{2,1,0:T(8,128)(2,1)S(1)}, u32[]{:S(2)}, u32[]{:S(2)}) %all-to-all-start) | async-done | bytes 524320 | tf_op jit(solution)/shard_map/all_to_all | solution.py:175
  62.1 0.0 collective-permute-done.refs_0_
  62.1 0.0 collective-permute-done.1.refs_1_
  62.1 0.0 copy-done.3
  62.1 0.0 copy-done.4
  62.1 7.6 %attend.1 = bf16[32,64,128]{2,1,0:T(8,128)(2,1)S(1)} custom-call(s32[16]{0:T(128)S(1)} %copy-done.4, s32[2,16]{1,0:T(2,128)S(1)} %copy-done.3, bf16[32,64,128]{2,1,0:T(8,128)(2,1)S(1)} %all-to-all-done.query_ref, bf16[32,128,128]{2,1,0:T(8,128)(2,1)S(1)} %all-to-all-done.1.own_ref, bf16[4,128,128]{2,1,0:T(8,128)(2,1)S(1)} %collective-permute-done.refs_0_, ...), custom_call_target="tpu_custom_call" | custom-call | flops 2684354560 | bytes 2097152 | tf_op jit(solution)/shard_map/attend/pallas_call | solution.py:160
  69.7 20.3 %all_to_all.15.source = bf16[32,64,128]{2,1,0:T(8,128)(2,1)S(1)} all-to-all(bf16[32,64,128]{2,1,0:T(8,128)(2,1)S(1)} %attend.1), channel_id=1, replica_groups=mesh['shot'=16,'head'=32] {'head'}, dimensions={0} | all-to-all | bytes 1048576 | tf_op jit(solution)/shard_map/all_to_all | solution.py:175
  90.1 0.9 join_heads.1
Async XLA Ops:
  0.0 1.0 %copy-start.1 = (bf16[1,64,4096]{2,1,0:T(8,128)(2,1)S(1)}, bf16[1,64,4096]{2,1,0:T(8,128)(2,1)}, u32[]{:S(2)}) copy-start(bf16[1,64,4096]{2,1,0:T(8,128)(2,1)} %param.7) | copy-start | bytes 1572868
  1.0 1.0 %copy-start.2 = (bf16[1,64,4096]{2,1,0:T(8,128)(2,1)S(1)}, bf16[1,64,4096]{2,1,0:T(8,128)(2,1)}, u32[]{:S(2)}) copy-start(bf16[1,64,4096]{2,1,0:T(8,128)(2,1)} %param.8) | copy-start | bytes 1572868
  3.2 10.6 %copy-start = (bf16[1,64,4096]{2,1,0:T(8,128)(2,1)S(1)}, bf16[1,64,4096]{2,1,0:T(8,128)(2,1)}, u32[]{:S(2)}) copy-start(bf16[1,64,4096]{2,1,0:T(8,128)(2,1)} %param.6) | copy-start | bytes 1572868
  3.2 37.3 %all-to-all-start.1 = ((bf16[32,128,128]{2,1,0:T(8,128)(2,1)}), bf16[32,128,128]{2,1,0:T(8,128)(2,1)S(1)}, u32[]{:S(2)}, u32[]{:S(2)}) async-start(bf16[32,128,128]{2,1,0:T(8,128)(2,1)} %split_heads.3), calls=%async_computation.1 | async-start | bytes 2097152 | tf_op jit(solution)/shard_map/all_to_all | solution.py:175
  14.7 30.9 %copy-start.5 = (s32[2,16,2]{1,2,0:T(2,128)S(1)}, s32[2,16,2]{1,2,0:T(2,128)}, u32[]{:S(2)}) copy-start(s32[2,16,2]{1,2,0:T(2,128)} %param.11) | copy-start | bytes 772
  40.5 21.5 %all-to-all-start = ((bf16[32,64,128]{2,1,0:T(8,128)(2,1)}), bf16[32,64,128]{2,1,0:T(8,128)(2,1)S(1)}, u32[]{:S(2)}, u32[]{:S(2)}) async-start(bf16[32,64,128]{2,1,0:T(8,128)(2,1)} %split_heads.2), calls=%async_computation | async-start | bytes 1048576 | tf_op jit(solution)/shard_map/all_to_all | solution.py:175
  46.6 15.5 %copy-start.3 = (s32[2,16]{1,0:T(2,128)S(1)}, s32[2,16]{1,0:T(2,128)}, u32[]{:S(2)}) copy-start(s32[2,16]{1,0:T(2,128)} %links.1) | copy-start | bytes 388
  46.6 15.5 %copy-start.4 = (s32[16]{0:T(128)S(1)}, s32[16]{0:T(128)}, u32[]{:S(2)}) copy-start(s32[16]{0:T(128)} %lengths.1) | copy-start | bytes 196
  46.6 15.4 %collective-permute-start = (bf16[4,128,128]{2,1,0:T(8,128)(2,1)S(1)}, bf16[4,128,128]{2,1,0:T(8,128)(2,1)S(1)}, u32[]{:S(2)}, u32[]{:S(2)}) collective-permute-start(bf16[4,128,128]{2,1,0:T(8,128)(2,1)S(1)} %get-tuple-element.7), channel_id=1, source_target_pairs={{0,256},{32,288},{64,320},{96,352},{128,384},{160,416},{192,448},{... | collective-permute-start | bytes 393224 | tf_op jit(solution)/shard_map/ppermute | solution.py:180
  51.0 11.1 %collective-permute-start.1 = (bf16[4,128,128]{2,1,0:T(8,128)(2,1)S(1)}, bf16[4,128,128]{2,1,0:T(8,128)(2,1)S(1)}, u32[]{:S(2)}, u32[]{:S(2)}) collective-permute-start(bf16[4,128,128]{2,1,0:T(8,128)(2,1)S(1)} %get-tuple-element.8), channel_id=1, source_target_pairs={{0,128},{32,160},{64,192},{96,224},{128,0},{160,32},{192,64},{224,... | collective-permute-start | bytes 393224 | tf_op jit(solution)/shard_map/ppermute | solution.py:180

commit v2 on v1

--- a/solution.py
+++ b/solution.py
@@ -13,35 +13,69 @@
 ROUNDS = 2
 SHOTS = 16
 FAR = SEL * BLK
-SCALE = HEAD_DIM ** (-0.5)
-LOG2E = 1.4426950408889634
-NEG = -1e30
+FACTOR = HEAD_DIM ** (-0.5) * 1.4426950408889634
 CHUNK = 256
 SUB = 256
+HEADS_A_STEP = 4
 VMEM_BYTES = 24 << 20
 SMALL_BYTES = 6 << 20
+LARGE_BYTES = 60 << 20
 
 
 def split_heads_kernel(*refs):
-    *sources, out_ref = refs
-    heads, _, _ = out_ref.shape
-    rows = sources[0].shape[0]
-    for number, source in enumerate(sources):
-        for head in range(heads):
-            out_ref[head, number * rows : (number + 1) * rows, :] = source[
-                :, head * HEAD_DIM : (head + 1) * HEAD_DIM
-            ]
-
-
-def split_heads(*arrays):
+    count = len(refs) - 5
+    sources, out_ref, held, made, come, gone = refs[:count], *refs[count:]
+    rows = held.shape[1]
+    wide = HEADS_A_STEP * HEAD_DIM
+    steps = out_ref.shape[0] // HEADS_A_STEP
+    arrivals = [
+        [
+            pltpu.make_async_copy(
+                source.at[:, pl.ds(step * wide, wide)],
+                held.at[number, :, pl.ds(step * wide, wide)],
+                come.at[number, step],
+            )
+            for number, source in enumerate(sources)
+        ]
+        for step in range(steps)
+    ]
+    for step in arrivals:
+        for arrival in step:
+            arrival.start()
+    leaving = []
+    for step in range(steps):
+        place = pl.ds(step * HEADS_A_STEP, HEADS_A_STEP)
+        for number in range(count):
+            arrivals[step][number].wait()
+            for head in range(step * HEADS_A_STEP, (step + 1) * HEADS_A_STEP):
+                made[head, number * rows : (number + 1) * rows, :] = held[
+                    number, :, head * HEAD_DIM : (head + 1) * HEAD_DIM
+                ]
+        copy = pltpu.make_async_copy(made.at[place], out_ref.at[place], gone.at[step])
+        copy.start()
+        leaving.append(copy)
+    for copy in leaving:
+        copy.wait()
+
+
+def split_heads(*arrays, vmem_bytes=SMALL_BYTES):
+    count = len(arrays)
     rows, width = arrays[0].shape
     heads = width // HEAD_DIM
+    steps = heads // HEADS_A_STEP
+    shape = (heads, count * rows, HEAD_DIM)
     return pl.pallas_call(
         split_heads_kernel,
-        in_specs=[pl.BlockSpec(memory_space=pltpu.VMEM)] * len(arrays),
-        out_specs=pl.BlockSpec(memory_space=pltpu.VMEM),
-        out_shape=jax.ShapeDtypeStruct((heads, len(arrays) * rows, HEAD_DIM), jnp.bfloat16),
-        compiler_params=pltpu.CompilerParams(vmem_limit_bytes=SMALL_BYTES),
+        in_specs=[pl.BlockSpec(memory_space=pltpu.HBM)] * count,
+        out_specs=pl.BlockSpec(memory_space=pltpu.HBM),
+        out_shape=jax.ShapeDtypeStruct(shape, jnp.bfloat16),
+        scratch_shapes=[
+            pltpu.VMEM((count, rows, width), jnp.bfloat16),
+            pltpu.VMEM(shape, jnp.bfloat16),
+            pltpu.SemaphoreType.DMA((count, steps)),
+            pltpu.SemaphoreType.DMA((steps,)),
+        ],
+        compiler_params=pltpu.CompilerParams(vmem_limit_bytes=vmem_bytes),
         name="split_heads",
     )(*arrays)
 
@@ -91,31 +125,37 @@
 
 
 def attend_kernel(lengths, links, query_ref, own_ref, *refs):
-    *far_refs, out_ref, value_ref = refs
+    *far_refs, out_ref = refs
     shot = lax.axis_index("shot")
     length = lengths[shot]
     piece = query_ref.shape[1]
-    group = CHUNK // piece
-    lane = lax.broadcasted_iota(jnp.int32, (1, CHUNK), 1)
-    keys, bias = [], []
-
-    def add_keys(source, first, shift):
-        place = slice(first, first + group)
-        spot = slice(len(keys) * CHUNK, (len(keys) + 1) * CHUNK)
-        keys.append(source[place, 0:piece, :].reshape(CHUNK, HEAD_DIM))
-        value_ref[spot, :HEAD_DIM] = source[place, piece : 2 * piece, :].reshape(CHUNK, HEAD_DIM)
-        value_ref[spot, HEAD_DIM:] = jnp.ones((CHUNK, HEAD_DIM), jnp.bfloat16)
-        bias.append(shift)
-
-    for chunk in range(LMAX // CHUNK):
-        shift = None
-        if (chunk + 1) * CHUNK > LMIN:
-            shift = jnp.where(lane + chunk * CHUNK < length, 0.0, NEG).astype(jnp.float32)
-        add_keys(own_ref, chunk * group, shift)
+    group = BLK // piece
+    blocks = []
+    for block in range(LMAX // BLK):
+        live = None if (block + 1) * BLK <= LMIN else block * BLK < length
+        blocks.append((own_ref, block * group, live))
     for round_index, far_ref in enumerate(far_refs):
-        shift = jnp.where(links[round_index, shot] > 0, 0.0, NEG).astype(jnp.float32)
-        for chunk in range(FAR // CHUNK):
-            add_keys(far_ref, chunk * group, shift)
+        for pick in range(SEL):
+            blocks.append((far_ref, pick * group, links[round_index, shot] > 0))
+    chunks = [blocks[n : n + CHUNK // BLK] for n in range(0, len(blocks), CHUNK // BLK)]
+
+    def keys_of(chunk):
+        parts = []
+        for source, first, live in chunk:
+            part = source[first : first + group, 0:piece, :].reshape(BLK, HEAD_DIM)
+            if live is not None:
+                part = jnp.where(live, part, own_ref[0:group, 0:piece, :].reshape(BLK, HEAD_DIM))
+            parts.append(part)
+        key = jnp.concatenate(parts, axis=0)
+        return jnp.concatenate([key, key], axis=1)
+
+    def values_of(chunk):
+        parts = []
+        for source, first, live in chunk:
+            part = source[first : first + group, piece : 2 * piece, :].reshape(BLK, HEAD_DIM)
+            part = jnp.concatenate([part, jnp.ones_like(part)], axis=1)
+            parts.append(part if live is None else jnp.where(live, part, jnp.zeros_like(part)))
+        return jnp.concatenate(parts, axis=0)
 
     parts = LMAX // SUB
     scores, row_max = None, None
@@ -123,23 +163,23 @@
         new_scores, top, weighted = [], None, None
         if part < parts:
             place = slice(part * SUB // piece, (part + 1) * SUB // piece)
-            query = query_ref[place].reshape(SUB, HEAD_DIM)
-        for chunk, (key, shift) in enumerate(zip(keys, bias)):
+            scaled = query_ref[place].reshape(SUB, HEAD_DIM).astype(jnp.float32) * FACTOR
+            high = scaled.astype(jnp.bfloat16)
+            low = (scaled - high.astype(jnp.float32)).astype(jnp.bfloat16)
+            query = jnp.concatenate([high, low], axis=1)
+        for number, chunk in enumerate(chunks):
             if part < parts:
                 score = lax.dot_general(
-                    query, key, (((1,), (1,)), ((), ())), preferred_element_type=jnp.float32
+                    query,
+                    keys_of(chunk),
+                    (((1,), (1,)), ((), ())),
+                    preferred_element_type=jnp.float32,
                 )
-                if shift is not None:
-                    score = score + shift
                 new_scores.append(score)
                 top = score if top is None else jnp.maximum(top, score)
             if part > 0:
-                terms = jnp.exp2(scores[chunk] * (SCALE * LOG2E) - row_max)
-                product = jnp.dot(
-                    terms.astype(jnp.bfloat16),
-                    value_ref[chunk * CHUNK : (chunk + 1) * CHUNK, :],
-                    preferred_element_type=jnp.float32,
-                )
+                terms = jnp.exp2(scores[number] - row_max).astype(jnp.bfloat16)
+                product = jnp.dot(terms, values_of(chunk), preferred_element_type=jnp.float32)
                 weighted = product if weighted is None else weighted + product
         if part > 0:
             first = (part - 1) * SUB
@@ -150,7 +190,7 @@
                 SUB // piece, piece, HEAD_DIM
             )
         if part < parts:
-            scores, row_max = new_scores, jnp.max(top, axis=1, keepdims=True) * (SCALE * LOG2E)
+            scores, row_max = new_scores, jnp.max(top, axis=1, keepdims=True)
 
 
 def attend(lengths, links, query, own, *far):
@@ -162,7 +202,6 @@
         in_specs=[smem, smem] + [vmem] * (2 + ROUNDS),
         out_specs=vmem,
         out_shape=jax.ShapeDtypeStruct(query.shape, jnp.bfloat16),
-        scratch_shapes=[pltpu.VMEM((keys, 2 * HEAD_DIM), jnp.bfloat16)],
         compiler_params=pltpu.CompilerParams(vmem_limit_bytes=VMEM_BYTES),
         cost_estimate=pl.CostEstimate(
             flops=4 * LMAX * keys * HEAD_DIM, bytes_accessed=2 << 20, transcendentals=LMAX * keys
@@ -181,7 +220,7 @@
 
 
 def body(queries, key_rows, value_rows, shot_lengths, shot_links, block_select):
-    own = swap(split_heads(key_rows[0], value_rows[0]))
+    own = swap(split_heads(key_rows[0], value_rows[0], vmem_bytes=LARGE_BYTES))
     query = swap(split_heads(queries[0]))
     far = [
         from_partner(picked, SHOTS >> (round_index + 1))

time: 91.4 us -> 89.6 us (0.980)
  local copies, waits for them, and re-layouts: 2.19 us -> 0.11 us
    unnamed x13 -> x9, local copies, waits for them, and re-layouts: 2.19 us -> 0.11 us
    pallas_call x2, Pallas kernels: 2.04 us -> 3.15 us  [split_heads(): pl.pallas_call(split_heads_kernel, in_specs=[pl.BlockSpec(memory_space=pl...]
where the time goes in v2:
time: 89.6 us; the launch traced here: 89.2 us
  waiting for transfers between devices  34.5 us (39%)
  starting transfers between devices  22.3 us (25%)
  blocking collectives  20.4 us (23%)
  Pallas kernels  11.8 us (13%)
    all_to_all x2, waiting for transfers between devices, swap(): lax.all_to_all(array, 'head', split_axis=0, concat_axis=0, tiled=True)  34.5 us
    all_to_all x1, blocking collectives, swap(): lax.all_to_all(array, 'head', split_axis=0, concat_axis=0, tiled=True)  20.4 us
    all_to_all x2, starting transfers between devices, swap(): lax.all_to_all(array, 'head', split_axis=0, concat_axis=0, tiled=True)  15.7 us
    pallas_call x1, Pallas kernels, attend(): pl.pallas_call(attend_kernel, in_specs=[smem, smem] + [vmem] * (2 + ROUND...  6.9 us
    ppermute x2, starting transfers between devices, from_partner(): lax.ppermute(array, 'shot', [(low, low ^ bit) for low in range(count)])  6.59 us
    pallas_call x2, Pallas kernels, split_heads(): pl.pallas_call(split_heads_kernel, in_specs=[pl.BlockSpec(memory_space=pl...  3.15 us
  transfers between devices with their start and end apart: 4, of which 2 were waited for; matrix products, arithmetic and copies ran while one was open for 0% of the time, Pallas kernels for 2%

profile of v2, /device:TPU:1, one launch (start us, length us, event | category | flops | bytes accessed | tf_op | source)
XLA Modules:
  0.0 89.2 jit_solution(8358013279267072148)
XLA Ops:
  0.0 2.1 %split_heads.3 = bf16[32,128,128]{2,1,0:T(8,128)(2,1)} custom-call(bf16[64,4096]{1,0:T(8,128)(2,1)} %bitcast.5, bf16[64,4096]{1,0:T(8,128)(2,1)} %bitcast.6), custom_call_target="tpu_custom_call" | custom-call | tf_op jit(solution)/shard_map/split_heads/pallas_call | solution.py:67
  2.1 0.0 copy-start
  2.1 10.6 %all-to-all-start.1 = ((bf16[32,128,128]{2,1,0:T(8,128)(2,1)}), bf16[32,128,128]{2,1,0:T(8,128)(2,1)S(1)}, u32[]{:S(2)}, u32[]{:S(2)}) async-start(bf16[32,128,128]{2,1,0:T(8,128)(2,1)} %split_heads.3), calls=%async_computation.1 | async-start | bytes 2097152 | tf_op jit(solution)/shard_map/all_to_all | solution.py:214
  12.8 0.0 copy-done
  12.8 1.0 %split_heads.2 = bf16[32,64,128]{2,1,0:T(8,128)(2,1)} custom-call(bf16[64,4096]{1,0:T(8,128)(2,1)S(1)} %bitcast.4), custom_call_target="tpu_custom_call" | custom-call | tf_op jit(solution)/shard_map/split_heads/pallas_call | solution.py:67
  13.8 0.0 copy-start.3
  13.8 25.6 %all-to-all-done.1.own_ref = bf16[32,128,128]{2,1,0:T(8,128)(2,1)S(1)} async-done(((bf16[32,128,128]{2,1,0:T(8,128)(2,1)}), bf16[32,128,128]{2,1,0:T(8,128)(2,1)S(1)}, u32[]{:S(2)}, u32[]{:S(2)}) %all-to-all-start.1) | async-done | bytes 1048608 | tf_op jit(solution)/shard_map/all_to_all | solution.py:214
  39.4 5.1 %all-to-all-start = ((bf16[32,64,128]{2,1,0:T(8,128)(2,1)}), bf16[32,64,128]{2,1,0:T(8,128)(2,1)S(1)}, u32[]{:S(2)}, u32[]{:S(2)}) async-start(bf16[32,64,128]{2,1,0:T(8,128)(2,1)} %split_heads.2), calls=%async_computation | async-start | bytes 1048576 | tf_op jit(solution)/shard_map/all_to_all | solution.py:214
  44.6 0.0 copy-done.3
  44.6 0.1 copy.7.block_select
  44.7 0.8 pick_blocks.1
  45.5 0.0 copy-start.1
  45.5 0.0 copy-start.2
  45.5 4.4 %collective-permute-start = (bf16[4,128,128]{2,1,0:T(8,128)(2,1)S(1)}, bf16[4,128,128]{2,1,0:T(8,128)(2,1)S(1)}, u32[]{:S(2)}, u32[]{:S(2)}) collective-permute-start(bf16[4,128,128]{2,1,0:T(8,128)(2,1)S(1)} %get-tuple-element.7), channel_id=1, source_target_pairs={{0,256},{32,288},{64,320},{96,352},{128,384},{160,416},{192,448},{... | collective-permute-start | bytes 393224 | tf_op jit(solution)/shard_map/ppermute | solution.py:219
  49.9 2.2 %collective-permute-start.1 = (bf16[4,128,128]{2,1,0:T(8,128)(2,1)S(1)}, bf16[4,128,128]{2,1,0:T(8,128)(2,1)S(1)}, u32[]{:S(2)}, u32[]{:S(2)}) collective-permute-start(bf16[4,128,128]{2,1,0:T(8,128)(2,1)S(1)} %get-tuple-element.8), channel_id=1, source_target_pairs={{0,128},{32,160},{64,192},{96,224},{128,0},{160,32},{192,64},{224,... | collective-permute-start | bytes 393224 | tf_op jit(solution)/shard_map/ppermute | solution.py:219
  52.2 8.8 %all-to-all-done.query_ref = bf16[32,64,128]{2,1,0:T(8,128)(2,1)S(1)} async-done(((bf16[32,64,128]{2,1,0:T(8,128)(2,1)}), bf16[32,64,128]{2,1,0:T(8,128)(2,1)S(1)}, u32[]{:S(2)}, u32[]{:S(2)}) %all-to-all-start) | async-done | bytes 524320 | tf_op jit(solution)/shard_map/all_to_all | solution.py:214
  61.0 0.0 collective-permute-done.refs_0_
  61.0 0.0 collective-permute-done.1.refs_1_
  61.0 0.0 copy-done.1
  61.0 0.0 copy-done.2
  61.0 6.9 %attend.1 = bf16[32,64,128]{2,1,0:T(8,128)(2,1)S(1)} custom-call(s32[16]{0:T(128)S(1)} %copy-done.2, s32[2,16]{1,0:T(2,128)S(1)} %copy-done.1, bf16[32,64,128]{2,1,0:T(8,128)(2,1)S(1)} %all-to-all-done.query_ref, bf16[32,128,128]{2,1,0:T(8,128)(2,1)S(1)} %all-to-all-done.1.own_ref, bf16[4,128,128]{2,1,0:T(8,128)(2,1)S(1)} %collective-permute-done.refs_0_, ...), custom_call_target="tpu_custom_call" | custom-call | flops 2684354560 | bytes 2097152 | tf_op jit(solution)/shard_map/attend/pallas_call | solution.py:200
  67.9 20.4 %all_to_all.15.source = bf16[32,64,128]{2,1,0:T(8,128)(2,1)S(1)} all-to-all(bf16[32,64,128]{2,1,0:T(8,128)(2,1)S(1)} %attend.1), channel_id=1, replica_groups=mesh['shot'=16,'head'=32] {'head'}, dimensions={0} | all-to-all | bytes 1048576 | tf_op jit(solution)/shard_map/all_to_all | solution.py:214
  88.3 0.9 join_heads.1
Async XLA Ops:
  2.1 10.6 %copy-start = (bf16[1,64,4096]{2,1,0:T(8,128)(2,1)S(1)}, bf16[1,64,4096]{2,1,0:T(8,128)(2,1)}, u32[]{:S(2)}) copy-start(bf16[1,64,4096]{2,1,0:T(8,128)(2,1)} %param.6) | copy-start | bytes 1572868
  2.1 37.3 %all-to-all-start.1 = ((bf16[32,128,128]{2,1,0:T(8,128)(2,1)}), bf16[32,128,128]{2,1,0:T(8,128)(2,1)S(1)}, u32[]{:S(2)}, u32[]{:S(2)}) async-start(bf16[32,128,128]{2,1,0:T(8,128)(2,1)} %split_heads.3), calls=%async_computation.1 | async-start | bytes 2097152 | tf_op jit(solution)/shard_map/all_to_all | solution.py:214
  13.8 30.8 %copy-start.3 = (s32[2,16,2]{1,2,0:T(2,128)S(1)}, s32[2,16,2]{1,2,0:T(2,128)}, u32[]{:S(2)}) copy-start(s32[2,16,2]{1,2,0:T(2,128)} %param.11) | copy-start | bytes 772
  39.4 21.5 %all-to-all-start = ((bf16[32,64,128]{2,1,0:T(8,128)(2,1)}), bf16[32,64,128]{2,1,0:T(8,128)(2,1)S(1)}, u32[]{:S(2)}, u32[]{:S(2)}) async-start(bf16[32,64,128]{2,1,0:T(8,128)(2,1)} %split_heads.2), calls=%async_computation | async-start | bytes 1048576 | tf_op jit(solution)/shard_map/all_to_all | solution.py:214
  45.5 15.5 %copy-start.1 = (s32[2,16]{1,0:T(2,128)S(1)}, s32[2,16]{1,0:T(2,128)}, u32[]{:S(2)}) copy-start(s32[2,16]{1,0:T(2,128)} %links.1) | copy-start | bytes 388
  45.5 15.5 %copy-start.2 = (s32[16]{0:T(128)S(1)}, s32[16]{0:T(128)}, u32[]{:S(2)}) copy-start(s32[16]{0:T(128)} %lengths.1) | copy-start | bytes 196
  45.5 15.4 %collective-permute-start = (bf16[4,128,128]{2,1,0:T(8,128)(2,1)S(1)}, bf16[4,128,128]{2,1,0:T(8,128)(2,1)S(1)}, u32[]{:S(2)}, u32[]{:S(2)}) collective-permute-start(bf16[4,128,128]{2,1,0:T(8,128)(2,1)S(1)} %get-tuple-element.7), channel_id=1, source_target_pairs={{0,256},{32,288},{64,320},{96,352},{128,384},{160,416},{192,448},{... | collective-permute-start | bytes 393224 | tf_op jit(solution)/shard_map/ppermute | solution.py:219
  49.9 11.1 %collective-permute-start.1 = (bf16[4,128,128]{2,1,0:T(8,128)(2,1)S(1)}, bf16[4,128,128]{2,1,0:T(8,128)(2,1)S(1)}, u32[]{:S(2)}, u32[]{:S(2)}) collective-permute-start(bf16[4,128,128]{2,1,0:T(8,128)(2,1)S(1)} %get-tuple-element.8), channel_id=1, source_target_pairs={{0,128},{32,160},{64,192},{96,224},{128,0},{160,32},{192,64},{224,... | collective-permute-start | bytes 393224 | tf_op jit(solution)/shard_map/ppermute | solution.py:219

commit v3 on v2

--- a/solution.py
+++ b/solution.py
@@ -1,3 +1,5 @@
+import functools
+
 import jax
 import jax.numpy as jnp
 from jax import lax
@@ -80,6 +82,81 @@
     )(*arrays)
 
 
+def split_queries_kernel(source, *refs):
+    outs, held, come = refs[:4], refs[4], refs[5]
+    steps = come.shape[0]
+    wide = held.shape[1] // steps
+    copies = []
+    for step in range(steps):
+        lanes = pl.ds(step * wide, wide)
+        copy = pltpu.make_async_copy(source.at[:, lanes], held.at[:, lanes], come.at[step])
+        copy.start()
+        copies.append(copy)
+    for copy in copies:
+        copy.wait()
+    me = lax.axis_index("head")
+    for ry, out_ref in enumerate(outs):
+        for place in range(out_ref.shape[0]):
+            head = me ^ (8 * (place // 2) + 2 * ry + place % 2)
+            first = pl.multiple_of(head * HEAD_DIM, HEAD_DIM)
+            out_ref[place] = held[:, pl.ds(first, HEAD_DIM)]
+
+
+def split_queries(array):
+    rows, width = array.shape
+    shape = jax.ShapeDtypeStruct((width // HEAD_DIM // 4, rows, HEAD_DIM), jnp.bfloat16)
+    return pl.pallas_call(
+        split_queries_kernel,
+        in_specs=[pl.BlockSpec(memory_space=pltpu.HBM)],
+        out_specs=[pl.BlockSpec(memory_space=pltpu.VMEM)] * 4,
+        out_shape=[shape] * 4,
+        scratch_shapes=[pltpu.VMEM((rows, width), jnp.bfloat16), pltpu.SemaphoreType.DMA((4,))],
+        compiler_params=pltpu.CompilerParams(vmem_limit_bytes=SMALL_BYTES),
+        name="split_queries",
+    )(array)
+
+
+def pack_chips_kernel(*refs):
+    *by_y, out_ref = refs
+    me = lax.axis_index("head")
+    for rz in range(4):
+        for core in range(2):
+            spot = (me // 8 ^ rz) * 2 + (me % 2 ^ core)
+            for ry, source in enumerate(by_y):
+                out_ref[spot, ry] = source[2 * rz + core]
+
+
+def pack_chips(arrays):
+    vmem = pl.BlockSpec(memory_space=pltpu.VMEM)
+    return pl.pallas_call(
+        pack_chips_kernel,
+        in_specs=[vmem] * len(arrays),
+        out_specs=vmem,
+        out_shape=jax.ShapeDtypeStruct((8, len(arrays), *arrays[0].shape[1:]), jnp.bfloat16),
+        compiler_params=pltpu.CompilerParams(vmem_limit_bytes=SMALL_BYTES),
+        name="pack_chips",
+    )(*arrays)
+
+
+def from_head(array, flip):
+    count = lax.axis_size("head")
+    return lax.ppermute(array, "head", [(low, low ^ flip) for low in range(count)])
+
+
+def gather_queries(array):
+    near, *others = split_queries(array)
+    by_y = [near] + [from_head(part, 2 * ry) for ry, part in zip(range(1, 4), others)]
+    groups = [[z * 8 + 2 * y + core for z in range(4) for core in range(2)] for y in range(4)]
+    return lax.all_to_all(
+        pack_chips(by_y),
+        "head",
+        split_axis=0,
+        concat_axis=0,
+        tiled=True,
+        axis_index_groups=groups,
+    )
+
+
 def join_heads_kernel(source, out_ref):
     heads, _, _ = source.shape
     for head in range(heads):
@@ -124,11 +201,12 @@
     )(block_select, own)
 
 
-def attend_kernel(lengths, links, query_ref, own_ref, *refs):
-    *far_refs, out_ref = refs
-    shot = lax.axis_index("shot")
+def attend_kernel(lengths, links, own_ref, *refs):
+    query_ref, far_refs, out_ref = refs[0], refs[1:-1], refs[-1]
+    shot, me = lax.axis_index("shot"), lax.axis_index("head")
     length = lengths[shot]
-    piece = query_ref.shape[1]
+    _, held, piece, _ = query_ref.shape
+    count = SUB // piece
     group = BLK // piece
     blocks = []
     for block in range(LMAX // BLK):
@@ -162,8 +240,8 @@
     for part in range(parts + 1):
         new_scores, top, weighted = [], None, None
         if part < parts:
-            place = slice(part * SUB // piece, (part + 1) * SUB // piece)
-            scaled = query_ref[place].reshape(SUB, HEAD_DIM).astype(jnp.float32) * FACTOR
+            chip, first = part * count // held, part * count % held
+            scaled = query_ref[chip, first : first + count].reshape(SUB, HEAD_DIM).astype(jnp.float32) * FACTOR
             high = scaled.astype(jnp.bfloat16)
             low = (scaled - high.astype(jnp.float32)).astype(jnp.bfloat16)
             query = jnp.concatenate([high, low], axis=1)
@@ -182,32 +260,33 @@
                 product = jnp.dot(terms, values_of(chunk), preferred_element_type=jnp.float32)
                 weighted = product if weighted is None else weighted + product
         if part > 0:
-            first = (part - 1) * SUB
-            position = first + lax.broadcasted_iota(jnp.int32, (SUB, 1), 0)
             result = weighted[:, :HEAD_DIM] / weighted[:, HEAD_DIM : HEAD_DIM + 1]
-            result = jnp.where(position < length, result, 0.0).astype(jnp.bfloat16)
-            out_ref[first // piece : (first + SUB) // piece] = result.reshape(
-                SUB // piece, piece, HEAD_DIM
-            )
+            for number in range(count):
+                chip, place = divmod((part - 1) * count + number, held)
+                spot = chip // 2 * 8 + 2 * (me // 2 % held ^ place) + chip % 2
+                rows = result[number * piece : (number + 1) * piece]
+                rows = jnp.where(spot * piece < length, rows, 0.0)
+                out_ref[spot] = rows.astype(jnp.bfloat16)
         if part < parts:
             scores, row_max = new_scores, jnp.max(top, axis=1, keepdims=True)
 
 
-def attend(lengths, links, query, own, *far):
+def attend(lengths, links, own, query, far):
     keys = LMAX + ROUNDS * FAR
     smem = pl.BlockSpec(memory_space=pltpu.SMEM)
     vmem = pl.BlockSpec(memory_space=pltpu.VMEM)
+    pieces = own.shape[0], own.shape[1] // 2, HEAD_DIM
     return pl.pallas_call(
         attend_kernel,
         in_specs=[smem, smem] + [vmem] * (2 + ROUNDS),
         out_specs=vmem,
-        out_shape=jax.ShapeDtypeStruct(query.shape, jnp.bfloat16),
+        out_shape=jax.ShapeDtypeStruct(pieces, jnp.bfloat16),
         compiler_params=pltpu.CompilerParams(vmem_limit_bytes=VMEM_BYTES),
         cost_estimate=pl.CostEstimate(
             flops=4 * LMAX * keys * HEAD_DIM, bytes_accessed=2 << 20, transcendentals=LMAX * keys
         ),
         name="attend",
-    )(lengths, links, query, own, *far)
+    )(lengths, links, own, query, *far)
 
 
 def swap(array):
@@ -221,12 +300,12 @@
 
 def body(queries, key_rows, value_rows, shot_lengths, shot_links, block_select):
     own = swap(split_heads(key_rows[0], value_rows[0], vmem_bytes=LARGE_BYTES))
-    query = swap(split_heads(queries[0]))
+    query = gather_queries(queries[0])
     far = [
         from_partner(picked, SHOTS >> (round_index + 1))
         for round_index, picked in enumerate(pick_blocks(block_select, own))
     ]
-    result = attend(shot_lengths, shot_links, query, own, *far)
+    result = attend(shot_lengths, shot_links, own, query, far)
     return join_heads(swap(result))[None]
 
 

time: 89.6 us -> 87.8 us (0.980)
  waiting for transfers between devices: 34.5 us -> 22.8 us
  starting transfers between devices: 22.3 us -> 30.1 us
  blocking collectives: 20.4 us -> 22.2 us
    all_to_all x2 -> x1, waiting for transfers between devices: 34.5 us -> 4.7 us  [swap(): lax.all_to_all(array, 'head', split_axis=0, concat_axis=0, tiled=True)]
    ppermute x0 -> x3, waiting for transfers between devices: none -> 11.3 us  [from_head(): lax.ppermute(array, 'head', [(low, low ^ flip) for low in range(count)])]
    ppermute x0 -> x3, starting transfers between devices: none -> 9.58 us  [from_head(): lax.ppermute(array, 'head', [(low, low ^ flip) for low in range(count)])]
    all_to_all x0 -> x1, waiting for transfers between devices: none -> 6.88 us  [gather_queries(): lax.all_to_all(pack_chips(by_y), 'head', split_axis=0, concat_axis=0, til...]
    all_to_all x2 -> x1, starting transfers between devices: 15.7 us -> 10.6 us  [swap(): lax.all_to_all(array, 'head', split_axis=0, concat_axis=0, tiled=True)]
    all_to_all x0 -> x1, starting transfers between devices: none -> 3.45 us  [gather_queries(): lax.all_to_all(pack_chips(by_y), 'head', split_axis=0, concat_axis=0, til...]
    all_to_all x1, blocking collectives: 20.4 us -> 22.2 us  [swap(): lax.all_to_all(array, 'head', split_axis=0, concat_axis=0, tiled=True)]
    pallas_call x0 -> x2, Pallas kernels: none -> 1.11 us  [the longest x1 0.84 us: pack_chips(): pl.pallas_call(pack_chips_kernel, in_specs=[vmem] * len(arrays), out_spec...]
  transfers between devices with their start and end apart: 4 -> 7, of which waited for: 2 -> 5; matrix products, arithmetic and copies ran while one was open for 0% -> 0% of each run, Pallas kernels for 2% -> 2%
where the time goes in v3:
time: 87.8 us; the launch traced here: 87.2 us
  starting transfers between devices  30.1 us (34%)
  waiting for transfers between devices  22.8 us (26%)
  blocking collectives  22.2 us (25%)
  Pallas kernels  11.9 us (14%)
    all_to_all x1, blocking collectives, swap(): lax.all_to_all(array, 'head', split_axis=0, concat_axis=0, tiled=True)  22.2 us
    ppermute x3, waiting for transfers between devices, from_head(): lax.ppermute(array, 'head', [(low, low ^ flip) for low in range(count)])  11.3 us
    all_to_all x1, starting transfers between devices, swap(): lax.all_to_all(array, 'head', split_axis=0, concat_axis=0, tiled=True)  10.6 us
    ppermute x3, starting transfers between devices, from_head(): lax.ppermute(array, 'head', [(low, low ^ flip) for low in range(count)])  9.58 us
    pallas_call x1, Pallas kernels, attend(): pl.pallas_call(attend_kernel, in_specs=[smem, smem] + [vmem] * (2 + ROUND...  6.88 us
    all_to_all x1, waiting for transfers between devices, gather_queries(): lax.all_to_all(pack_chips(by_y), 'head', split_axis=0, concat_axis=0, til...  6.88 us
    ppermute x2, starting transfers between devices, from_partner(): lax.ppermute(array, 'shot', [(low, low ^ bit) for low in range(count)])  6.49 us
    all_to_all x1, waiting for transfers between devices, swap(): lax.all_to_all(array, 'head', split_axis=0, concat_axis=0, tiled=True)  4.7 us
  transfers between devices with their start and end apart: 7, of which 5 were waited for; matrix products, arithmetic and copies ran while one was open for 0% of the time, Pallas kernels for 2%

profile of v3, /device:TPU:1, one launch (start us, length us, event | category | flops | bytes accessed | tf_op | source)
XLA Modules:
  0.0 87.2 jit_solution(7634952432675657311)
XLA Ops:
  0.0 2.1 %split_heads.1 = bf16[32,128,128]{2,1,0:T(8,128)(2,1)} custom-call(bf16[64,4096]{1,0:T(8,128)(2,1)} %bitcast.5, bf16[64,4096]{1,0:T(8,128)(2,1)} %bitcast.6), custom_call_target="tpu_custom_call" | custom-call | tf_op jit(solution)/shard_map/split_heads/pallas_call | solution.py:69
  2.2 0.0 copy-start
  2.2 10.6 %all-to-all-start = ((bf16[32,128,128]{2,1,0:T(8,128)(2,1)}), bf16[32,128,128]{2,1,0:T(8,128)(2,1)S(1)}, u32[]{:S(2)}, u32[]{:S(2)}) async-start(bf16[32,128,128]{2,1,0:T(8,128)(2,1)} %split_heads.1), calls=%async_computation | async-start | bytes 2097152 | tf_op jit(solution)/shard_map/all_to_all | solution.py:293
  12.8 0.0 copy-done
  12.8 0.3 split_queries.1
  13.1 3.3 %collective-permute-start = (bf16[8,64,128]{2,1,0:T(8,128)(2,1)S(1)}, bf16[8,64,128]{2,1,0:T(8,128)(2,1)S(1)}, u32[]{:S(2)}, u32[]{:S(2)}) collective-permute-start(bf16[8,64,128]{2,1,0:T(8,128)(2,1)S(1)} %get-tuple-element.12), channel_id=1, source_target_pairs={{0,2},{1,3},{2,0},{3,1},{4,6},{5,7},{6,4},{7,5},{8,10},{9,11},{10,... | collective-permute-start | bytes 393224 | tf_op jit(solution)/shard_map/ppermute | solution.py:143
  16.4 4.3 %collective-permute-start.1 = (bf16[8,64,128]{2,1,0:T(8,128)(2,1)S(1)}, bf16[8,64,128]{2,1,0:T(8,128)(2,1)S(1)}, u32[]{:S(2)}, u32[]{:S(2)}) collective-permute-start(bf16[8,64,128]{2,1,0:T(8,128)(2,1)S(1)} %get-tuple-element.13), channel_id=1, source_target_pairs={{0,4},{1,5},{2,6},{3,7},{4,0},{5,1},{6,2},{7,3},{8,12},{9,13},{10,... | collective-permute-start | bytes 393224 | tf_op jit(solution)/shard_map/ppermute | solution.py:143
  20.7 2.0 %collective-permute-start.2 = (bf16[8,64,128]{2,1,0:T(8,128)(2,1)S(1)}, bf16[8,64,128]{2,1,0:T(8,128)(2,1)S(1)}, u32[]{:S(2)}, u32[]{:S(2)}) collective-permute-start(bf16[8,64,128]{2,1,0:T(8,128)(2,1)S(1)} %get-tuple-element.14), channel_id=1, source_target_pairs={{0,6},{1,7},{2,4},{3,5},{4,2},{5,3},{6,0},{7,1},{8,14},{9,15},{10,... | collective-permute-start | bytes 393224 | tf_op jit(solution)/shard_map/ppermute | solution.py:143
  22.7 2.7 %collective-permute-done.refs_1_ = bf16[8,64,128]{2,1,0:T(8,128)(2,1)S(1)} collective-permute-done((bf16[8,64,128]{2,1,0:T(8,128)(2,1)S(1)}, bf16[8,64,128]{2,1,0:T(8,128)(2,1)S(1)}, u32[]{:S(2)}, u32[]{:S(2)}) %collective-permute-start) | collective-permute-done | bytes 131104 | tf_op jit(solution)/shard_map/ppermute | solution.py:143
  25.4 5.9 %collective-permute-done.1.refs_2_ = bf16[8,64,128]{2,1,0:T(8,128)(2,1)S(1)} collective-permute-done((bf16[8,64,128]{2,1,0:T(8,128)(2,1)S(1)}, bf16[8,64,128]{2,1,0:T(8,128)(2,1)S(1)}, u32[]{:S(2)}, u32[]{:S(2)}) %collective-permute-start.1) | collective-permute-done | bytes 131104 | tf_op jit(solution)/shard_map/ppermute | solution.py:143
  31.3 2.6 %collective-permute-done.2.refs_3_ = bf16[8,64,128]{2,1,0:T(8,128)(2,1)S(1)} collective-permute-done((bf16[8,64,128]{2,1,0:T(8,128)(2,1)S(1)}, bf16[8,64,128]{2,1,0:T(8,128)(2,1)S(1)}, u32[]{:S(2)}, u32[]{:S(2)}) %collective-permute-start.2) | collective-permute-done | bytes 131104 | tf_op jit(solution)/shard_map/ppermute | solution.py:143
  33.9 0.8 pack_chips.1
  34.8 0.0 copy-start.3
  34.8 4.7 %all-to-all-done.own_ref = bf16[32,128,128]{2,1,0:T(8,128)(2,1)S(1)} async-done(((bf16[32,128,128]{2,1,0:T(8,128)(2,1)}), bf16[32,128,128]{2,1,0:T(8,128)(2,1)S(1)}, u32[]{:S(2)}, u32[]{:S(2)}) %all-to-all-start) | async-done | bytes 1048608 | tf_op jit(solution)/shard_map/all_to_all | solution.py:293
  39.5 3.4 %all-to-all-start.1 = ((bf16[8,4,64,128]{3,2,1,0:T(8,128)(2,1)}), bf16[8,4,64,128]{3,2,1,0:T(8,128)(2,1)S(1)}, u32[]{:S(2)}, u32[]{:S(2)}) async-start(bf16[8,4,64,128]{3,2,1,0:T(8,128)(2,1)} %pack_chips.1), calls=%async_computation.1 | async-start | bytes 1048576 | tf_op jit(solution)/shard_map/all_to_all | solution.py:150
  42.9 0.0 copy-done.3
  42.9 0.1 copy.7.block_select
  43.0 0.8 pick_blocks.1
  43.9 0.0 copy-start.1
  43.9 0.0 copy-start.2
  43.9 4.3 %collective-permute-start.3 = (bf16[4,128,128]{2,1,0:T(8,128)(2,1)S(1)}, bf16[4,128,128]{2,1,0:T(8,128)(2,1)S(1)}, u32[]{:S(2)}, u32[]{:S(2)}) collective-permute-start(bf16[4,128,128]{2,1,0:T(8,128)(2,1)S(1)} %get-tuple-element.15), channel_id=1, source_target_pairs={{0,256},{32,288},{64,320},{96,352},{128,384},{160,416},{192,448},{... | collective-permute-start | bytes 393224 | tf_op jit(solution)/shard_map/ppermute | solution.py:298
  48.2 2.2 %collective-permute-start.4 = (bf16[4,128,128]{2,1,0:T(8,128)(2,1)S(1)}, bf16[4,128,128]{2,1,0:T(8,128)(2,1)S(1)}, u32[]{:S(2)}, u32[]{:S(2)}) collective-permute-start(bf16[4,128,128]{2,1,0:T(8,128)(2,1)S(1)} %get-tuple-element.16), channel_id=1, source_target_pairs={{0,128},{32,160},{64,192},{96,224},{128,0},{160,32},{192,64},{224,... | collective-permute-start | bytes 393224 | tf_op jit(solution)/shard_map/ppermute | solution.py:298
  50.4 6.9 %all-to-all-done.1.refs_0_ = bf16[8,4,64,128]{3,2,1,0:T(8,128)(2,1)S(1)} async-done(((bf16[8,4,64,128]{3,2,1,0:T(8,128)(2,1)}), bf16[8,4,64,128]{3,2,1,0:T(8,128)(2,1)S(1)}, u32[]{:S(2)}, u32[]{:S(2)}) %all-to-all-start.1) | async-done | bytes 524320 | tf_op jit(solution)/shard_map/all_to_all | solution.py:150
  57.3 0.0 collective-permute-done.3.refs_1_
  57.3 0.0 collective-permute-done.4.refs_2_
  57.3 0.0 copy-done.1
  57.3 0.0 copy-done.2
  57.3 6.9 %attend.1 = bf16[32,64,128]{2,1,0:T(8,128)(2,1)S(1)} custom-call(s32[16]{0:T(128)S(1)} %copy-done.2, s32[2,16]{1,0:T(2,128)S(1)} %copy-done.1, bf16[32,128,128]{2,1,0:T(8,128)(2,1)S(1)} %all-to-all-done.own_ref, bf16[8,4,64,128]{3,2,1,0:T(8,128)(2,1)S(1)} %all-to-all-done.1.refs_0_, bf16[4,128,128]{2,1,0:T(8,128)(2,1)S(1)} %collective-permute-done.3.refs_1_, ...), custom_call_target="tpu_custom_call" | custom-call | flops 2684354560 | bytes 2097152 | tf_op jit(solution)/shard_map/attend/pallas_call | solution.py:279
  64.2 22.2 %all_to_all.15.source = bf16[32,64,128]{2,1,0:T(8,128)(2,1)S(1)} all-to-all(bf16[32,64,128]{2,1,0:T(8,128)(2,1)S(1)} %attend.1), channel_id=1, replica_groups=mesh['shot'=16,'head'=32] {'head'}, dimensions={0} | all-to-all | bytes 1048576 | tf_op jit(solution)/shard_map/all_to_all | solution.py:293
  86.4 0.9 %join_heads.1 = bf16[64,4096]{1,0:T(8,128)(2,1)} custom-call(bf16[32,64,128]{2,1,0:T(8,128)(2,1)S(1)} %all_to_all.15.source), custom_call_target="tpu_custom_call" | custom-call | tf_op jit(solution)/shard_map/join_heads/pallas_call | solution.py:168
Async XLA Ops:
  2.2 10.6 %copy-start = (bf16[1,64,4096]{2,1,0:T(8,128)(2,1)S(1)}, bf16[1,64,4096]{2,1,0:T(8,128)(2,1)}, u32[]{:S(2)}) copy-start(bf16[1,64,4096]{2,1,0:T(8,128)(2,1)} %param.6) | copy-start | bytes 1572868
  2.2 37.3 %all-to-all-start = ((bf16[32,128,128]{2,1,0:T(8,128)(2,1)}), bf16[32,128,128]{2,1,0:T(8,128)(2,1)S(1)}, u32[]{:S(2)}, u32[]{:S(2)}) async-start(bf16[32,128,128]{2,1,0:T(8,128)(2,1)} %split_heads.1), calls=%async_computation | async-start | bytes 2097152 | tf_op jit(solution)/shard_map/all_to_all | solution.py:293
  13.1 12.3 %collective-permute-start = (bf16[8,64,128]{2,1,0:T(8,128)(2,1)S(1)}, bf16[8,64,128]{2,1,0:T(8,128)(2,1)S(1)}, u32[]{:S(2)}, u32[]{:S(2)}) collective-permute-start(bf16[8,64,128]{2,1,0:T(8,128)(2,1)S(1)} %get-tuple-element.12), channel_id=1, source_target_pairs={{0,2},{1,3},{2,0},{3,1},{4,6},{5,7},{6,4},{7,5},{8,10},{9,11},{10,... | collective-permute-start | bytes 393224 | tf_op jit(solution)/shard_map/ppermute | solution.py:143
  16.4 15.0 %collective-permute-start.1 = (bf16[8,64,128]{2,1,0:T(8,128)(2,1)S(1)}, bf16[8,64,128]{2,1,0:T(8,128)(2,1)S(1)}, u32[]{:S(2)}, u32[]{:S(2)}) collective-permute-start(bf16[8,64,128]{2,1,0:T(8,128)(2,1)S(1)} %get-tuple-element.13), channel_id=1, source_target_pairs={{0,4},{1,5},{2,6},{3,7},{4,0},{5,1},{6,2},{7,3},{8,12},{9,13},{10,... | collective-permute-start | bytes 393224 | tf_op jit(solution)/shard_map/ppermute | solution.py:143
  20.7 13.2 %collective-permute-start.2 = (bf16[8,64,128]{2,1,0:T(8,128)(2,1)S(1)}, bf16[8,64,128]{2,1,0:T(8,128)(2,1)S(1)}, u32[]{:S(2)}, u32[]{:S(2)}) collective-permute-start(bf16[8,64,128]{2,1,0:T(8,128)(2,1)S(1)} %get-tuple-element.14), channel_id=1, source_target_pairs={{0,6},{1,7},{2,4},{3,5},{4,2},{5,3},{6,0},{7,1},{8,14},{9,15},{10,... | collective-permute-start | bytes 393224 | tf_op jit(solution)/shard_map/ppermute | solution.py:143
  34.8 8.2 %copy-start.3 = (s32[2,16,2]{1,2,0:T(2,128)S(1)}, s32[2,16,2]{1,2,0:T(2,128)}, u32[]{:S(2)}) copy-start(s32[2,16,2]{1,2,0:T(2,128)} %param.11) | copy-start | bytes 772
  39.5 17.8 %all-to-all-start.1 = ((bf16[8,4,64,128]{3,2,1,0:T(8,128)(2,1)}), bf16[8,4,64,128]{3,2,1,0:T(8,128)(2,1)S(1)}, u32[]{:S(2)}, u32[]{:S(2)}) async-start(bf16[8,4,64,128]{3,2,1,0:T(8,128)(2,1)} %pack_chips.1), calls=%async_computation.1 | async-start | bytes 1048576 | tf_op jit(solution)/shard_map/all_to_all | solution.py:150
  43.9 13.4 %copy-start.1 = (s32[2,16]{1,0:T(2,128)S(1)}, s32[2,16]{1,0:T(2,128)}, u32[]{:S(2)}) copy-start(s32[2,16]{1,0:T(2,128)} %links.1) | copy-start | bytes 388
  43.9 13.4 %copy-start.2 = (s32[16]{0:T(128)S(1)}, s32[16]{0:T(128)}, u32[]{:S(2)}) copy-start(s32[16]{0:T(128)} %lengths.1) | copy-start | bytes 196
  43.9 13.4 %collective-permute-start.3 = (bf16[4,128,128]{2,1,0:T(8,128)(2,1)S(1)}, bf16[4,128,128]{2,1,0:T(8,128)(2,1)S(1)}, u32[]{:S(2)}, u32[]{:S(2)}) collective-permute-start(bf16[4,128,128]{2,1,0:T(8,128)(2,1)S(1)} %get-tuple-element.15), channel_id=1, source_target_pairs={{0,256},{32,288},{64,320},{96,352},{128,384},{160,416},{192,448},{... | collective-permute-start | bytes 393224 | tf_op jit(solution)/shard_map/ppermute | solution.py:298
  48.2 9.1 %collective-permute-start.4 = (bf16[4,128,128]{2,1,0:T(8,128)(2,1)S(1)}, bf16[4,128,128]{2,1,0:T(8,128)(2,1)S(1)}, u32[]{:S(2)}, u32[]{:S(2)}) collective-permute-start(bf16[4,128,128]{2,1,0:T(8,128)(2,1)S(1)} %get-tuple-element.16), channel_id=1, source_target_pairs={{0,128},{32,160},{64,192},{96,224},{128,0},{160,32},{192,64},{224,... | collective-permute-start | bytes 393224 | tf_op jit(solution)/shard_map/ppermute | solution.py:298

commit v4 on v3

--- a/solution.py
+++ b/solution.py
@@ -17,9 +17,9 @@
 FAR = SEL * BLK
 FACTOR = HEAD_DIM ** (-0.5) * 1.4426950408889634
 CHUNK = 256
-SUB = 256
-HEADS_A_STEP = 4
-VMEM_BYTES = 24 << 20
+SUB = 1024
+HEADS_A_STEP = 2
+VMEM_BYTES = 46 << 20
 SMALL_BYTES = 6 << 20
 LARGE_BYTES = 60 << 20
 
@@ -240,8 +240,8 @@
     for part in range(parts + 1):
         new_scores, top, weighted = [], None, None
         if part < parts:
-            chip, first = part * count // held, part * count % held
-            scaled = query_ref[chip, first : first + count].reshape(SUB, HEAD_DIM).astype(jnp.float32) * FACTOR
+            chips = slice(part * count // held, (part + 1) * count // held)
+            scaled = query_ref[chips].reshape(SUB, HEAD_DIM).astype(jnp.float32) * FACTOR
             high = scaled.astype(jnp.bfloat16)
             low = (scaled - high.astype(jnp.float32)).astype(jnp.bfloat16)
             query = jnp.concatenate([high, low], axis=1)

time: 87.8 us -> 87.5 us (level)
  no operation moved by 1% of the time
where the time goes in v4:
time: 87.5 us; the launch traced here: 86.9 us
  starting transfers between devices  30.1 us (34%)
  waiting for transfers between devices  22.8 us (26%)
  blocking collectives  22.2 us (25%)
  Pallas kernels  11.5 us (13%)
    all_to_all x1, blocking collectives, swap(): lax.all_to_all(array, 'head', split_axis=0, concat_axis=0, tiled=True)  22.2 us
    ppermute x3, waiting for transfers between devices, from_head(): lax.ppermute(array, 'head', [(low, low ^ flip) for low in range(count)])  11.3 us
    all_to_all x1, starting transfers between devices, swap(): lax.all_to_all(array, 'head', split_axis=0, concat_axis=0, tiled=True)  10.6 us
    ppermute x3, starting transfers between devices, from_head(): lax.ppermute(array, 'head', [(low, low ^ flip) for low in range(count)])  9.58 us
    all_to_all x1, waiting for transfers between devices, gather_queries(): lax.all_to_all(pack_chips(by_y), 'head', split_axis=0, concat_axis=0, til...  6.88 us
    ppermute x2, starting transfers between devices, from_partner(): lax.ppermute(array, 'shot', [(low, low ^ bit) for low in range(count)])  6.49 us
    pallas_call x1, Pallas kernels, attend(): pl.pallas_call(attend_kernel, in_specs=[smem, smem] + [vmem] * (2 + ROUND...  6.43 us
    all_to_all x1, waiting for transfers between devices, swap(): lax.all_to_all(array, 'head', split_axis=0, concat_axis=0, tiled=True)  4.7 us
  transfers between devices with their start and end apart: 7, of which 5 were waited for; matrix products, arithmetic and copies ran while one was open for 0% of the time, Pallas kernels for 2%

profile of v4, /device:TPU:1, one launch (start us, length us, event | category | flops | bytes accessed | tf_op | source)
XLA Modules:
  0.0 86.9 jit_solution(5935177482765158680)
XLA Ops:
  0.0 2.3 %split_heads.1 = bf16[32,128,128]{2,1,0:T(8,128)(2,1)} custom-call(bf16[64,4096]{1,0:T(8,128)(2,1)} %bitcast.5, bf16[64,4096]{1,0:T(8,128)(2,1)} %bitcast.6), custom_call_target="tpu_custom_call" | custom-call | tf_op jit(solution)/shard_map/split_heads/pallas_call | solution.py:69
  2.3 0.0 copy-start
  2.3 10.6 %all-to-all-start = ((bf16[32,128,128]{2,1,0:T(8,128)(2,1)}), bf16[32,128,128]{2,1,0:T(8,128)(2,1)S(1)}, u32[]{:S(2)}, u32[]{:S(2)}) async-start(bf16[32,128,128]{2,1,0:T(8,128)(2,1)} %split_heads.1), calls=%async_computation | async-start | bytes 2097152 | tf_op jit(solution)/shard_map/all_to_all | solution.py:293
  12.9 0.0 copy-done
  12.9 0.3 split_queries.1
  13.2 3.3 %collective-permute-start = (bf16[8,64,128]{2,1,0:T(8,128)(2,1)S(1)}, bf16[8,64,128]{2,1,0:T(8,128)(2,1)S(1)}, u32[]{:S(2)}, u32[]{:S(2)}) collective-permute-start(bf16[8,64,128]{2,1,0:T(8,128)(2,1)S(1)} %get-tuple-element.12), channel_id=1, source_target_pairs={{0,2},{1,3},{2,0},{3,1},{4,6},{5,7},{6,4},{7,5},{8,10},{9,11},{10,... | collective-permute-start | bytes 393224 | tf_op jit(solution)/shard_map/ppermute | solution.py:143
  16.5 4.3 %collective-permute-start.1 = (bf16[8,64,128]{2,1,0:T(8,128)(2,1)S(1)}, bf16[8,64,128]{2,1,0:T(8,128)(2,1)S(1)}, u32[]{:S(2)}, u32[]{:S(2)}) collective-permute-start(bf16[8,64,128]{2,1,0:T(8,128)(2,1)S(1)} %get-tuple-element.13), channel_id=1, source_target_pairs={{0,4},{1,5},{2,6},{3,7},{4,0},{5,1},{6,2},{7,3},{8,12},{9,13},{10,... | collective-permute-start | bytes 393224 | tf_op jit(solution)/shard_map/ppermute | solution.py:143
  20.8 2.0 %collective-permute-start.2 = (bf16[8,64,128]{2,1,0:T(8,128)(2,1)S(1)}, bf16[8,64,128]{2,1,0:T(8,128)(2,1)S(1)}, u32[]{:S(2)}, u32[]{:S(2)}) collective-permute-start(bf16[8,64,128]{2,1,0:T(8,128)(2,1)S(1)} %get-tuple-element.14), channel_id=1, source_target_pairs={{0,6},{1,7},{2,4},{3,5},{4,2},{5,3},{6,0},{7,1},{8,14},{9,15},{10,... | collective-permute-start | bytes 393224 | tf_op jit(solution)/shard_map/ppermute | solution.py:143
  22.8 2.7 %collective-permute-done.refs_1_ = bf16[8,64,128]{2,1,0:T(8,128)(2,1)S(1)} collective-permute-done((bf16[8,64,128]{2,1,0:T(8,128)(2,1)S(1)}, bf16[8,64,128]{2,1,0:T(8,128)(2,1)S(1)}, u32[]{:S(2)}, u32[]{:S(2)}) %collective-permute-start) | collective-permute-done | bytes 131104 | tf_op jit(solution)/shard_map/ppermute | solution.py:143
  25.5 5.9 %collective-permute-done.1.refs_2_ = bf16[8,64,128]{2,1,0:T(8,128)(2,1)S(1)} collective-permute-done((bf16[8,64,128]{2,1,0:T(8,128)(2,1)S(1)}, bf16[8,64,128]{2,1,0:T(8,128)(2,1)S(1)}, u32[]{:S(2)}, u32[]{:S(2)}) %collective-permute-start.1) | collective-permute-done | bytes 131104 | tf_op jit(solution)/shard_map/ppermute | solution.py:143
  31.5 2.6 %collective-permute-done.2.refs_3_ = bf16[8,64,128]{2,1,0:T(8,128)(2,1)S(1)} collective-permute-done((bf16[8,64,128]{2,1,0:T(8,128)(2,1)S(1)}, bf16[8,64,128]{2,1,0:T(8,128)(2,1)S(1)}, u32[]{:S(2)}, u32[]{:S(2)}) %collective-permute-start.2) | collective-permute-done | bytes 131104 | tf_op jit(solution)/shard_map/ppermute | solution.py:143
  34.1 0.8 pack_chips.1
  34.9 0.0 copy-start.3
  34.9 4.7 %all-to-all-done.own_ref = bf16[32,128,128]{2,1,0:T(8,128)(2,1)S(1)} async-done(((bf16[32,128,128]{2,1,0:T(8,128)(2,1)}), bf16[32,128,128]{2,1,0:T(8,128)(2,1)S(1)}, u32[]{:S(2)}, u32[]{:S(2)}) %all-to-all-start) | async-done | bytes 1048608 | tf_op jit(solution)/shard_map/all_to_all | solution.py:293
  39.6 3.4 %all-to-all-start.1 = ((bf16[8,4,64,128]{3,2,1,0:T(8,128)(2,1)}), bf16[8,4,64,128]{3,2,1,0:T(8,128)(2,1)S(1)}, u32[]{:S(2)}, u32[]{:S(2)}) async-start(bf16[8,4,64,128]{3,2,1,0:T(8,128)(2,1)} %pack_chips.1), calls=%async_computation.1 | async-start | bytes 1048576 | tf_op jit(solution)/shard_map/all_to_all | solution.py:150
  43.0 0.0 copy-done.3
  43.1 0.1 copy.7.block_select
  43.1 0.8 pick_blocks.1
  44.0 0.0 copy-start.1
  44.0 0.0 copy-start.2
  44.0 4.3 %collective-permute-start.3 = (bf16[4,128,128]{2,1,0:T(8,128)(2,1)S(1)}, bf16[4,128,128]{2,1,0:T(8,128)(2,1)S(1)}, u32[]{:S(2)}, u32[]{:S(2)}) collective-permute-start(bf16[4,128,128]{2,1,0:T(8,128)(2,1)S(1)} %get-tuple-element.15), channel_id=1, source_target_pairs={{0,256},{32,288},{64,320},{96,352},{128,384},{160,416},{192,448},{... | collective-permute-start | bytes 393224 | tf_op jit(solution)/shard_map/ppermute | solution.py:298
  48.3 2.2 %collective-permute-start.4 = (bf16[4,128,128]{2,1,0:T(8,128)(2,1)S(1)}, bf16[4,128,128]{2,1,0:T(8,128)(2,1)S(1)}, u32[]{:S(2)}, u32[]{:S(2)}) collective-permute-start(bf16[4,128,128]{2,1,0:T(8,128)(2,1)S(1)} %get-tuple-element.16), channel_id=1, source_target_pairs={{0,128},{32,160},{64,192},{96,224},{128,0},{160,32},{192,64},{224,... | collective-permute-start | bytes 393224 | tf_op jit(solution)/shard_map/ppermute | solution.py:298
  50.5 6.9 %all-to-all-done.1.refs_0_ = bf16[8,4,64,128]{3,2,1,0:T(8,128)(2,1)S(1)} async-done(((bf16[8,4,64,128]{3,2,1,0:T(8,128)(2,1)}), bf16[8,4,64,128]{3,2,1,0:T(8,128)(2,1)S(1)}, u32[]{:S(2)}, u32[]{:S(2)}) %all-to-all-start.1) | async-done | bytes 524320 | tf_op jit(solution)/shard_map/all_to_all | solution.py:150
  57.4 0.0 collective-permute-done.3.refs_1_
  57.4 0.0 collective-permute-done.4.refs_2_
  57.4 0.0 copy-done.1
  57.4 0.0 copy-done.2
  57.4 6.4 %attend.1 = bf16[32,64,128]{2,1,0:T(8,128)(2,1)S(1)} custom-call(s32[16]{0:T(128)S(1)} %copy-done.2, s32[2,16]{1,0:T(2,128)S(1)} %copy-done.1, bf16[32,128,128]{2,1,0:T(8,128)(2,1)S(1)} %all-to-all-done.own_ref, bf16[8,4,64,128]{3,2,1,0:T(8,128)(2,1)S(1)} %all-to-all-done.1.refs_0_, bf16[4,128,128]{2,1,0:T(8,128)(2,1)S(1)} %collective-permute-done.3.refs_1_, ...), custom_call_target="tpu_custom_call" | custom-call | flops 2684354560 | bytes 2097152 | tf_op jit(solution)/shard_map/attend/pallas_call | solution.py:279
  63.8 22.2 %all_to_all.15.source = bf16[32,64,128]{2,1,0:T(8,128)(2,1)S(1)} all-to-all(bf16[32,64,128]{2,1,0:T(8,128)(2,1)S(1)} %attend.1), channel_id=1, replica_groups=mesh['shot'=16,'head'=32] {'head'}, dimensions={0} | all-to-all | bytes 1048576 | tf_op jit(solution)/shard_map/all_to_all | solution.py:293
  86.0 0.9 %join_heads.1 = bf16[64,4096]{1,0:T(8,128)(2,1)} custom-call(bf16[32,64,128]{2,1,0:T(8,128)(2,1)S(1)} %all_to_all.15.source), custom_call_target="tpu_custom_call" | custom-call | tf_op jit(solution)/shard_map/join_heads/pallas_call | solution.py:168
Async XLA Ops:
  2.3 10.6 %copy-start = (bf16[1,64,4096]{2,1,0:T(8,128)(2,1)S(1)}, bf16[1,64,4096]{2,1,0:T(8,128)(2,1)}, u32[]{:S(2)}) copy-start(bf16[1,64,4096]{2,1,0:T(8,128)(2,1)} %param.6) | copy-start | bytes 1572868
  2.3 37.3 %all-to-all-start = ((bf16[32,128,128]{2,1,0:T(8,128)(2,1)}), bf16[32,128,128]{2,1,0:T(8,128)(2,1)S(1)}, u32[]{:S(2)}, u32[]{:S(2)}) async-start(bf16[32,128,128]{2,1,0:T(8,128)(2,1)} %split_heads.1), calls=%async_computation | async-start | bytes 2097152 | tf_op jit(solution)/shard_map/all_to_all | solution.py:293
  13.2 12.3 %collective-permute-start = (bf16[8,64,128]{2,1,0:T(8,128)(2,1)S(1)}, bf16[8,64,128]{2,1,0:T(8,128)(2,1)S(1)}, u32[]{:S(2)}, u32[]{:S(2)}) collective-permute-start(bf16[8,64,128]{2,1,0:T(8,128)(2,1)S(1)} %get-tuple-element.12), channel_id=1, source_target_pairs={{0,2},{1,3},{2,0},{3,1},{4,6},{5,7},{6,4},{7,5},{8,10},{9,11},{10,... | collective-permute-start | bytes 393224 | tf_op jit(solution)/shard_map/ppermute | solution.py:143
  16.5 15.0 %collective-permute-start.1 = (bf16[8,64,128]{2,1,0:T(8,128)(2,1)S(1)}, bf16[8,64,128]{2,1,0:T(8,128)(2,1)S(1)}, u32[]{:S(2)}, u32[]{:S(2)}) collective-permute-start(bf16[8,64,128]{2,1,0:T(8,128)(2,1)S(1)} %get-tuple-element.13), channel_id=1, source_target_pairs={{0,4},{1,5},{2,6},{3,7},{4,0},{5,1},{6,2},{7,3},{8,12},{9,13},{10,... | collective-permute-start | bytes 393224 | tf_op jit(solution)/shard_map/ppermute | solution.py:143
  20.8 13.2 %collective-permute-start.2 = (bf16[8,64,128]{2,1,0:T(8,128)(2,1)S(1)}, bf16[8,64,128]{2,1,0:T(8,128)(2,1)S(1)}, u32[]{:S(2)}, u32[]{:S(2)}) collective-permute-start(bf16[8,64,128]{2,1,0:T(8,128)(2,1)S(1)} %get-tuple-element.14), channel_id=1, source_target_pairs={{0,6},{1,7},{2,4},{3,5},{4,2},{5,3},{6,0},{7,1},{8,14},{9,15},{10,... | collective-permute-start | bytes 393224 | tf_op jit(solution)/shard_map/ppermute | solution.py:143
  34.9 8.2 %copy-start.3 = (s32[2,16,2]{1,2,0:T(2,128)S(1)}, s32[2,16,2]{1,2,0:T(2,128)}, u32[]{:S(2)}) copy-start(s32[2,16,2]{1,2,0:T(2,128)} %param.11) | copy-start | bytes 772
  39.6 17.8 %all-to-all-start.1 = ((bf16[8,4,64,128]{3,2,1,0:T(8,128)(2,1)}), bf16[8,4,64,128]{3,2,1,0:T(8,128)(2,1)S(1)}, u32[]{:S(2)}, u32[]{:S(2)}) async-start(bf16[8,4,64,128]{3,2,1,0:T(8,128)(2,1)} %pack_chips.1), calls=%async_computation.1 | async-start | bytes 1048576 | tf_op jit(solution)/shard_map/all_to_all | solution.py:150
  44.0 13.4 %copy-start.1 = (s32[2,16]{1,0:T(2,128)S(1)}, s32[2,16]{1,0:T(2,128)}, u32[]{:S(2)}) copy-start(s32[2,16]{1,0:T(2,128)} %links.1) | copy-start | bytes 388
  44.0 13.4 %copy-start.2 = (s32[16]{0:T(128)S(1)}, s32[16]{0:T(128)}, u32[]{:S(2)}) copy-start(s32[16]{0:T(128)} %lengths.1) | copy-start | bytes 196
  44.0 13.4 %collective-permute-start.3 = (bf16[4,128,128]{2,1,0:T(8,128)(2,1)S(1)}, bf16[4,128,128]{2,1,0:T(8,128)(2,1)S(1)}, u32[]{:S(2)}, u32[]{:S(2)}) collective-permute-start(bf16[4,128,128]{2,1,0:T(8,128)(2,1)S(1)} %get-tuple-element.15), channel_id=1, source_target_pairs={{0,256},{32,288},{64,320},{96,352},{128,384},{160,416},{192,448},{... | collective-permute-start | bytes 393224 | tf_op jit(solution)/shard_map/ppermute | solution.py:298
  48.3 9.1 %collective-permute-start.4 = (bf16[4,128,128]{2,1,0:T(8,128)(2,1)S(1)}, bf16[4,128,128]{2,1,0:T(8,128)(2,1)S(1)}, u32[]{:S(2)}, u32[]{:S(2)}) collective-permute-start(bf16[4,128,128]{2,1,0:T(8,128)(2,1)S(1)} %get-tuple-element.16), channel_id=1, source_target_pairs={{0,128},{32,160},{64,192},{96,224},{128,0},{160,32},{192,64},{224,... | collective-permute-start | bytes 393224 | tf_op jit(solution)/shard_map/ppermute | solution.py:298

commit v5 on v3

--- a/solution.py
+++ b/solution.py
@@ -17,9 +17,9 @@
 FAR = SEL * BLK
 FACTOR = HEAD_DIM ** (-0.5) * 1.4426950408889634
 CHUNK = 256
-SUB = 256
+EARLY = 512
 HEADS_A_STEP = 4
-VMEM_BYTES = 24 << 20
+VMEM_BYTES = 28 << 20
 SMALL_BYTES = 6 << 20
 LARGE_BYTES = 60 << 20
 
@@ -116,6 +116,28 @@
     )(array)
 
 
+def pack_kernel(*refs, plan):
+    sources, outs = refs[: len(refs) - len(plan)], refs[len(refs) - len(plan) :]
+    for out_ref, pieces in zip(outs, plan):
+        for place, (number, piece) in enumerate(pieces):
+            out_ref[place] = sources[number][piece]
+
+
+def pack(arrays, plan):
+    vmem = pl.BlockSpec(memory_space=pltpu.VMEM)
+    return pl.pallas_call(
+        functools.partial(pack_kernel, plan=plan),
+        in_specs=[vmem] * len(arrays),
+        out_specs=[vmem] * len(plan),
+        out_shape=[
+            jax.ShapeDtypeStruct((len(pieces),) + arrays[0].shape[1:], jnp.bfloat16)
+            for pieces in plan
+        ],
+        compiler_params=pltpu.CompilerParams(vmem_limit_bytes=SMALL_BYTES),
+        name="pack",
+    )(*arrays)
+
+
 def pack_chips_kernel(*refs):
     *by_y, out_ref = refs
     me = lax.axis_index("head")
@@ -147,7 +169,8 @@
     near, *others = split_queries(array)
     by_y = [near] + [from_head(part, 2 * ry) for ry, part in zip(range(1, 4), others)]
     groups = [[z * 8 + 2 * y + core for z in range(4) for core in range(2)] for y in range(4)]
-    return lax.all_to_all(
+    keep, send = pack(by_y, [[(ry, core) for ry in range(4)] for core in range(2)])
+    rest = lax.all_to_all(
         pack_chips(by_y),
         "head",
         split_axis=0,
@@ -155,6 +178,7 @@
         tiled=True,
         axis_index_groups=groups,
     )
+    return keep, from_head(send, 1), rest
 
 
 def join_heads_kernel(source, out_ref):
@@ -201,92 +225,174 @@
     )(block_select, own)
 
 
-def attend_kernel(lengths, links, own_ref, *refs):
-    query_ref, far_refs, out_ref = refs[0], refs[1:-1], refs[-1]
-    shot, me = lax.axis_index("shot"), lax.axis_index("head")
-    length = lengths[shot]
-    _, held, piece, _ = query_ref.shape
-    count = SUB // piece
-    group = BLK // piece
+def keys_of(blocks, piece, spare):
+    parts = []
+    for source, first, live in blocks:
+        place = slice(first, first + BLK // piece)
+        part = source[place, 0:piece, :].reshape(BLK, HEAD_DIM)
+        if live is not None:
+            part = jnp.where(live, part, spare[0 : BLK // piece, 0:piece, :].reshape(BLK, HEAD_DIM))
+        parts.append(part)
+    key = jnp.concatenate(parts, axis=0)
+    return jnp.concatenate([key, key], axis=1)
+
+
+def values_of(blocks, piece):
+    parts = []
+    for source, first, live in blocks:
+        place = slice(first, first + BLK // piece)
+        part = source[place, piece : 2 * piece, :].reshape(BLK, HEAD_DIM)
+        part = jnp.concatenate([part, jnp.ones_like(part)], axis=1)
+        parts.append(part if live is None else jnp.where(live, part, jnp.zeros_like(part)))
+    return jnp.concatenate(parts, axis=0)
+
+
+def own_blocks(own_ref, piece, length):
     blocks = []
     for block in range(LMAX // BLK):
         live = None if (block + 1) * BLK <= LMIN else block * BLK < length
-        blocks.append((own_ref, block * group, live))
-    for round_index, far_ref in enumerate(far_refs):
-        for pick in range(SEL):
-            blocks.append((far_ref, pick * group, links[round_index, shot] > 0))
-    chunks = [blocks[n : n + CHUNK // BLK] for n in range(0, len(blocks), CHUNK // BLK)]
-
-    def keys_of(chunk):
-        parts = []
-        for source, first, live in chunk:
-            part = source[first : first + group, 0:piece, :].reshape(BLK, HEAD_DIM)
-            if live is not None:
-                part = jnp.where(live, part, own_ref[0:group, 0:piece, :].reshape(BLK, HEAD_DIM))
-            parts.append(part)
-        key = jnp.concatenate(parts, axis=0)
-        return jnp.concatenate([key, key], axis=1)
-
-    def values_of(chunk):
-        parts = []
-        for source, first, live in chunk:
-            part = source[first : first + group, piece : 2 * piece, :].reshape(BLK, HEAD_DIM)
-            part = jnp.concatenate([part, jnp.ones_like(part)], axis=1)
-            parts.append(part if live is None else jnp.where(live, part, jnp.zeros_like(part)))
-        return jnp.concatenate(parts, axis=0)
-
-    parts = LMAX // SUB
-    scores, row_max = None, None
-    for part in range(parts + 1):
-        new_scores, top, weighted = [], None, None
-        if part < parts:
-            chip, first = part * count // held, part * count % held
-            scaled = query_ref[chip, first : first + count].reshape(SUB, HEAD_DIM).astype(jnp.float32) * FACTOR
+        blocks.append((own_ref, block * (BLK // piece), live))
+    return blocks
+
+
+def attend_items(items, piece, spare):
+    per_chunk = CHUNK // BLK
+    scores, row_max, before = [], None, None
+    for item in items + [None]:
+        new_scores, top, weighted, chunks = [], None, None, []
+        if item is not None:
+            queries, blocks, floor, _ = item
+            scaled = queries().astype(jnp.float32) * FACTOR
             high = scaled.astype(jnp.bfloat16)
             low = (scaled - high.astype(jnp.float32)).astype(jnp.bfloat16)
             query = jnp.concatenate([high, low], axis=1)
-        for number, chunk in enumerate(chunks):
-            if part < parts:
+            chunks = [blocks[n : n + per_chunk] for n in range(0, len(blocks), per_chunk)]
+        for number in range(max(len(chunks), len(scores))):
+            if number < len(chunks):
                 score = lax.dot_general(
                     query,
-                    keys_of(chunk),
+                    keys_of(chunks[number], piece, spare),
                     (((1,), (1,)), ((), ())),
                     preferred_element_type=jnp.float32,
                 )
                 new_scores.append(score)
                 top = score if top is None else jnp.maximum(top, score)
-            if part > 0:
+            if number < len(scores):
                 terms = jnp.exp2(scores[number] - row_max).astype(jnp.bfloat16)
-                product = jnp.dot(terms, values_of(chunk), preferred_element_type=jnp.float32)
+                product = jnp.dot(
+                    terms, values_of(before[0][number], piece), preferred_element_type=jnp.float32
+                )
                 weighted = product if weighted is None else weighted + product
-        if part > 0:
-            result = weighted[:, :HEAD_DIM] / weighted[:, HEAD_DIM : HEAD_DIM + 1]
-            for number in range(count):
-                chip, place = divmod((part - 1) * count + number, held)
-                spot = chip // 2 * 8 + 2 * (me // 2 % held ^ place) + chip % 2
-                rows = result[number * piece : (number + 1) * piece]
-                rows = jnp.where(spot * piece < length, rows, 0.0)
-                out_ref[spot] = rows.astype(jnp.bfloat16)
-        if part < parts:
-            scores, row_max = new_scores, jnp.max(top, axis=1, keepdims=True)
-
-
-def attend(lengths, links, own, query, far):
-    keys = LMAX + ROUNDS * FAR
-    smem = pl.BlockSpec(memory_space=pltpu.SMEM)
-    vmem = pl.BlockSpec(memory_space=pltpu.VMEM)
-    pieces = own.shape[0], own.shape[1] // 2, HEAD_DIM
-    return pl.pallas_call(
-        attend_kernel,
-        in_specs=[smem, smem] + [vmem] * (2 + ROUNDS),
+        if before is not None:
+            before[1](weighted, row_max)
+        if item is not None:
+            scores, row_max = new_scores, floor(jnp.max(top, axis=1, keepdims=True))
+            before = (chunks, item[3])
+
+
+def early_queries(keep_ref, come_ref):
+    both = jnp.concatenate([keep_ref[...], come_ref[...]], axis=0)
+    return both.reshape(EARLY, HEAD_DIM)
+
+
+def attend_early_kernel(lengths, links, own_ref, keep_ref, come_ref, sum_ref, max_ref):
+    piece = own_ref.shape[1] // 2
+    blocks = own_blocks(own_ref, piece, lengths[lax.axis_index("shot")])
+
+    def item(source, place):
+        def finish(weighted, row_max):
+            sum_ref[place, :] = weighted
+            max_ref[place, :] = jnp.broadcast_to(row_max, (weighted.shape[0], HEAD_DIM))
+
+        def queries():
+            return source[...].reshape(EARLY // 2, HEAD_DIM)
+
+        return queries, blocks, lambda top: top, finish
+
+    halves = slice(0, EARLY // 2), slice(EARLY // 2, EARLY)
+    items = [item(source, place) for source, place in zip((keep_ref, come_ref), halves)]
+    attend_items(items, piece, own_ref)
+
+
+def attend_late_kernel(lengths, links, own_ref, query_ref, keep_ref, come_ref, *refs):
+    sum_ref, max_ref, *far_refs, out_ref = refs
+    shot, me = lax.axis_index("shot"), lax.axis_index("head")
+    length = lengths[shot]
+    piece = own_ref.shape[1] // 2
+    far = []
+    for round_index, far_ref in enumerate(far_refs):
+        for pick in range(SEL):
+            far.append((far_ref, pick * (BLK // piece), links[round_index, shot] > 0))
+    every = own_blocks(own_ref, piece, length) + far
+
+    def store(weighted, spots):
+        result = weighted[:, :HEAD_DIM] / weighted[:, HEAD_DIM : HEAD_DIM + 1]
+        for number, spot in enumerate(spots):
+            rows = result[number * piece : (number + 1) * piece]
+            out_ref[spot] = jnp.where(spot * piece < length, rows, 0.0).astype(jnp.bfloat16)
+
+    def finish_early(weighted, row_max):
+        kept = jnp.exp2(max_ref[...] - row_max)
+        kept = sum_ref[...] * jnp.concatenate([kept, kept], axis=1)
+        store(weighted + kept, [me ^ (2 * ry + core) for core in range(2) for ry in range(4)])
+
+    def late_item(chips):
+        spots = [
+            (me // 8 ^ rz) * 8 + 2 * (me // 2 % 4 ^ k) + core for rz, core in chips for k in range(4)
+        ]
+
+        def queries():
+            loads = [query_ref[(me // 8 ^ rz) * 2 + core] for rz, core in chips]
+            return jnp.concatenate(loads, axis=0).reshape(len(spots) * piece, HEAD_DIM)
+
+        return queries, every, lambda top: top, lambda weighted, _: store(weighted, spots)
+
+    early = (
+        functools.partial(early_queries, keep_ref, come_ref),
+        far,
+        lambda top: jnp.maximum(top, max_ref[:, 0:1]),
+        finish_early,
+    )
+    chips = [(rz, core) for rz in range(1, 4) for core in range(2)]
+    attend_items([early, late_item(chips[:3]), late_item(chips[3:])], piece, own_ref)
+
+
+def attend_cost(queries, keys):
+    return pl.CostEstimate(
+        flops=4 * queries * keys * HEAD_DIM,
+        bytes_accessed=2 << 20,
+        transcendentals=queries * keys,
+    )
+
+
+def attend_early(lengths, links, own, keep, come):
+    smem, vmem = pl.BlockSpec(memory_space=pltpu.SMEM), pl.BlockSpec(memory_space=pltpu.VMEM)
+    return pl.pallas_call(
+        attend_early_kernel,
+        in_specs=[smem, smem] + [vmem] * 3,
+        out_specs=[vmem] * 2,
+        out_shape=[
+            jax.ShapeDtypeStruct((EARLY, 2 * HEAD_DIM), jnp.float32),
+            jax.ShapeDtypeStruct((EARLY, HEAD_DIM), jnp.float32),
+        ],
+        compiler_params=pltpu.CompilerParams(vmem_limit_bytes=12 << 20),
+        cost_estimate=attend_cost(EARLY, LMAX),
+        name="attend_early",
+    )(lengths, links, own, keep, come)
+
+
+def attend_late(lengths, links, own, rest, keep, come, sums, tops, far):
+    smem, vmem = pl.BlockSpec(memory_space=pltpu.SMEM), pl.BlockSpec(memory_space=pltpu.VMEM)
+    shape = (own.shape[0], own.shape[1] // 2, HEAD_DIM)
+    return pl.pallas_call(
+        attend_late_kernel,
+        in_specs=[smem, smem] + [vmem] * (6 + ROUNDS),
         out_specs=vmem,
-        out_shape=jax.ShapeDtypeStruct(pieces, jnp.bfloat16),
+        out_shape=jax.ShapeDtypeStruct(shape, jnp.bfloat16),
         compiler_params=pltpu.CompilerParams(vmem_limit_bytes=VMEM_BYTES),
-        cost_estimate=pl.CostEstimate(
-            flops=4 * LMAX * keys * HEAD_DIM, bytes_accessed=2 << 20, transcendentals=LMAX * keys
-        ),
-        name="attend",
-    )(lengths, links, own, query, *far)
+        cost_estimate=attend_cost(LMAX - EARLY, LMAX + ROUNDS * FAR),
+        name="attend_late",
+    )(lengths, links, own, rest, keep, come, sums, tops, *far)
 
 
 def swap(array):
@@ -300,12 +406,13 @@
 
 def body(queries, key_rows, value_rows, shot_lengths, shot_links, block_select):
     own = swap(split_heads(key_rows[0], value_rows[0], vmem_bytes=LARGE_BYTES))
-    query = gather_queries(queries[0])
+    keep, come, rest = gather_queries(queries[0])
     far = [
         from_partner(picked, SHOTS >> (round_index + 1))
         for round_index, picked in enumerate(pick_blocks(block_select, own))
     ]
-    result = attend(shot_lengths, shot_links, own, query, far)
+    sums, tops = attend_early(shot_lengths, shot_links, own, keep, come)
+    result = attend_late(shot_lengths, shot_links, own, rest, keep, come, sums, tops, far)
     return join_heads(swap(result))[None]
 
 

time: 87.8 us -> 86.8 us (0.989)
  waiting for transfers between devices: 22.8 us -> 18.4 us
  starting transfers between devices: 30.1 us -> 32.6 us
    all_to_all x1, waiting for transfers between devices: 6.88 us -> 1.53 us  [gather_queries(): lax.all_to_all(pack_chips(by_y), 'head', split_axis=0, concat_axis=0, til...]
    ppermute x3 -> x4, starting transfers between devices: 9.58 us -> 12 us  [from_head(): lax.ppermute(array, 'head', [(low, low ^ flip) for low in range(count)])]
    ppermute x3 -> x4, waiting for transfers between devices: 11.3 us -> 12.1 us  [from_head(): lax.ppermute(array, 'head', [(low, low ^ flip) for low in range(count)])]
    pallas_call x1 -> x3, Pallas kernels: 6.88 us -> 7.41 us  [the longest x1 5.41 us: attend_late(): pl.pallas_call(attend_late_kernel, in_specs=[smem, smem] + [vmem] * (6 +...]
  transfers between devices with their start and end apart: 7 -> 8, of which waited for: 5 -> 6; matrix products, arithmetic and copies ran while one was open for 0% -> 0% of each run, Pallas kernels for 2% -> 5%
where the time goes in v5:
time: 86.8 us; the launch traced here: 86.2 us
  starting transfers between devices  32.6 us (38%)
  blocking collectives  22.6 us (26%)
  waiting for transfers between devices  18.4 us (21%)
  Pallas kernels  12.4 us (14%)
    all_to_all x1, blocking collectives, swap(): lax.all_to_all(array, 'head', split_axis=0, concat_axis=0, tiled=True)  22.6 us
    ppermute x4, waiting for transfers between devices, from_head(): lax.ppermute(array, 'head', [(low, low ^ flip) for low in range(count)])  12.1 us
    ppermute x4, starting transfers between devices, from_head(): lax.ppermute(array, 'head', [(low, low ^ flip) for low in range(count)])  12 us
    all_to_all x1, starting transfers between devices, swap(): lax.all_to_all(array, 'head', split_axis=0, concat_axis=0, tiled=True)  10.6 us
    ppermute x2, starting transfers between devices, from_partner(): lax.ppermute(array, 'shot', [(low, low ^ bit) for low in range(count)])  6.49 us
    pallas_call x1, Pallas kernels, attend_late(): pl.pallas_call(attend_late_kernel, in_specs=[smem, smem] + [vmem] * (6 +...  5.41 us
    all_to_all x1, waiting for transfers between devices, swap(): lax.all_to_all(array, 'head', split_axis=0, concat_axis=0, tiled=True)  4.7 us
    all_to_all x1, starting transfers between devices, gather_queries(): lax.all_to_all(pack_chips(by_y), 'head', split_axis=0, concat_axis=0, til...  3.45 us
  transfers between devices with their start and end apart: 8, of which 6 were waited for; matrix products, arithmetic and copies ran while one was open for 0% of the time, Pallas kernels for 5%

profile of v5, /device:TPU:1, one launch (start us, length us, event | category | flops | bytes accessed | tf_op | source)
XLA Modules:
  0.0 86.2 jit_solution(7779344278627359296)
XLA Ops:
  0.0 2.1 %split_heads.1 = bf16[32,128,128]{2,1,0:T(8,128)(2,1)} custom-call(bf16[64,4096]{1,0:T(8,128)(2,1)} %bitcast.5, bf16[64,4096]{1,0:T(8,128)(2,1)} %bitcast.6), custom_call_target="tpu_custom_call" | custom-call | tf_op jit(solution)/shard_map/split_heads/pallas_call | solution.py:69
  2.2 0.0 copy-start
  2.2 10.6 %all-to-all-start = ((bf16[32,128,128]{2,1,0:T(8,128)(2,1)}), bf16[32,128,128]{2,1,0:T(8,128)(2,1)S(1)}, u32[]{:S(2)}, u32[]{:S(2)}) async-start(bf16[32,128,128]{2,1,0:T(8,128)(2,1)} %split_heads.1), calls=%async_computation | async-start | bytes 2097152 | tf_op jit(solution)/shard_map/all_to_all | solution.py:399
  12.8 0.0 copy-done
  12.8 0.3 split_queries.1
  13.1 3.3 %collective-permute-start = (bf16[8,64,128]{2,1,0:T(8,128)(2,1)S(1)}, bf16[8,64,128]{2,1,0:T(8,128)(2,1)S(1)}, u32[]{:S(2)}, u32[]{:S(2)}) collective-permute-start(bf16[8,64,128]{2,1,0:T(8,128)(2,1)S(1)} %get-tuple-element.16), channel_id=1, source_target_pairs={{0,2},{1,3},{2,0},{3,1},{4,6},{5,7},{6,4},{7,5},{8,10},{9,11},{10,... | collective-permute-start | bytes 393224 | tf_op jit(solution)/shard_map/ppermute | solution.py:165
  16.4 4.3 %collective-permute-start.1 = (bf16[8,64,128]{2,1,0:T(8,128)(2,1)S(1)}, bf16[8,64,128]{2,1,0:T(8,128)(2,1)S(1)}, u32[]{:S(2)}, u32[]{:S(2)}) collective-permute-start(bf16[8,64,128]{2,1,0:T(8,128)(2,1)S(1)} %get-tuple-element.17), channel_id=1, source_target_pairs={{0,4},{1,5},{2,6},{3,7},{4,0},{5,1},{6,2},{7,3},{8,12},{9,13},{10,... | collective-permute-start | bytes 393224 | tf_op jit(solution)/shard_map/ppermute | solution.py:165
  20.7 2.0 %collective-permute-start.2 = (bf16[8,64,128]{2,1,0:T(8,128)(2,1)S(1)}, bf16[8,64,128]{2,1,0:T(8,128)(2,1)S(1)}, u32[]{:S(2)}, u32[]{:S(2)}) collective-permute-start(bf16[8,64,128]{2,1,0:T(8,128)(2,1)S(1)} %get-tuple-element.18), channel_id=1, source_target_pairs={{0,6},{1,7},{2,4},{3,5},{4,2},{5,3},{6,0},{7,1},{8,14},{9,15},{10,... | collective-permute-start | bytes 393224 | tf_op jit(solution)/shard_map/ppermute | solution.py:165
  22.7 2.7 %collective-permute-done.refs_1_ = bf16[8,64,128]{2,1,0:T(8,128)(2,1)S(1)} collective-permute-done((bf16[8,64,128]{2,1,0:T(8,128)(2,1)S(1)}, bf16[8,64,128]{2,1,0:T(8,128)(2,1)S(1)}, u32[]{:S(2)}, u32[]{:S(2)}) %collective-permute-start) | collective-permute-done | bytes 131104 | tf_op jit(solution)/shard_map/ppermute | solution.py:165
  25.4 5.9 %collective-permute-done.1.refs_2_ = bf16[8,64,128]{2,1,0:T(8,128)(2,1)S(1)} collective-permute-done((bf16[8,64,128]{2,1,0:T(8,128)(2,1)S(1)}, bf16[8,64,128]{2,1,0:T(8,128)(2,1)S(1)}, u32[]{:S(2)}, u32[]{:S(2)}) %collective-permute-start.1) | collective-permute-done | bytes 131104 | tf_op jit(solution)/shard_map/ppermute | solution.py:165
  31.3 2.6 %collective-permute-done.2.refs_3_ = bf16[8,64,128]{2,1,0:T(8,128)(2,1)S(1)} collective-permute-done((bf16[8,64,128]{2,1,0:T(8,128)(2,1)S(1)}, bf16[8,64,128]{2,1,0:T(8,128)(2,1)S(1)}, u32[]{:S(2)}, u32[]{:S(2)}) %collective-permute-start.2) | collective-permute-done | bytes 131104 | tf_op jit(solution)/shard_map/ppermute | solution.py:165
  33.9 0.8 pack_chips.1
  34.8 4.7 %all-to-all-done.own_ref = bf16[32,128,128]{2,1,0:T(8,128)(2,1)S(1)} async-done(((bf16[32,128,128]{2,1,0:T(8,128)(2,1)}), bf16[32,128,128]{2,1,0:T(8,128)(2,1)S(1)}, u32[]{:S(2)}, u32[]{:S(2)}) %all-to-all-start) | async-done | bytes 1048608 | tf_op jit(solution)/shard_map/all_to_all | solution.py:399
  39.5 3.4 %all-to-all-start.1 = ((bf16[8,4,64,128]{3,2,1,0:T(8,128)(2,1)}), bf16[8,4,64,128]{3,2,1,0:T(8,128)(2,1)S(1)}, u32[]{:S(2)}, u32[]{:S(2)}) async-start(bf16[8,4,64,128]{3,2,1,0:T(8,128)(2,1)} %pack_chips.1), calls=%async_computation.1 | async-start | bytes 1048576 | tf_op jit(solution)/shard_map/all_to_all | solution.py:173
  42.9 0.0 copy-done.3
  42.9 0.1 copy.7.block_select
  43.0 0.8 pick_blocks.1
  43.9 4.3 %collective-permute-start.4 = (bf16[4,128,128]{2,1,0:T(8,128)(2,1)S(1)}, bf16[4,128,128]{2,1,0:T(8,128)(2,1)S(1)}, u32[]{:S(2)}, u32[]{:S(2)}) collective-permute-start(bf16[4,128,128]{2,1,0:T(8,128)(2,1)S(1)} %get-tuple-element.23), channel_id=1, source_target_pairs={{0,256},{32,288},{64,320},{96,352},{128,384},{160,416},{192,448},{... | collective-permute-start | bytes 393224 | tf_op jit(solution)/shard_map/ppermute | solution.py:404
  48.1 2.2 %collective-permute-start.5 = (bf16[4,128,128]{2,1,0:T(8,128)(2,1)S(1)}, bf16[4,128,128]{2,1,0:T(8,128)(2,1)S(1)}, u32[]{:S(2)}, u32[]{:S(2)}) collective-permute-start(bf16[4,128,128]{2,1,0:T(8,128)(2,1)S(1)} %get-tuple-element.24), channel_id=1, source_target_pairs={{0,128},{32,160},{64,192},{96,224},{128,0},{160,32},{192,64},{224,... | collective-permute-start | bytes 393224 | tf_op jit(solution)/shard_map/ppermute | solution.py:404
  50.4 0.0 copy-start.1
  50.4 0.0 copy-start.2
  50.4 2.4 %collective-permute-start.3 = (bf16[4,64,128]{2,1,0:T(8,128)(2,1)S(1)}, bf16[4,64,128]{2,1,0:T(8,128)(2,1)S(1)}, u32[]{:S(2)}, u32[]{:S(2)}) collective-permute-start(bf16[4,64,128]{2,1,0:T(8,128)(2,1)S(1)} %get-tuple-element.20), channel_id=1, source_target_pairs={{0,1},{1,0},{2,3},{3,2},{4,5},{5,4},{6,7},{7,6},{8,9},{9,8},{10,11... | collective-permute-start | bytes 196616 | tf_op jit(solution)/shard_map/ppermute | solution.py:165
  52.9 0.9 %collective-permute-done.3.come_ref = bf16[4,64,128]{2,1,0:T(8,128)(2,1)S(1)} collective-permute-done((bf16[4,64,128]{2,1,0:T(8,128)(2,1)S(1)}, bf16[4,64,128]{2,1,0:T(8,128)(2,1)S(1)}, u32[]{:S(2)}, u32[]{:S(2)}) %collective-permute-start.3) | collective-permute-done | bytes 65568 | tf_op jit(solution)/shard_map/ppermute | solution.py:165
  53.7 0.0 copy-done.1
  53.7 0.0 copy-done.2
  53.7 2.0 %attend_early.1 = (f32[512,256]{1,0:T(8,128)S(1)}, f32[512,128]{1,0:T(8,128)S(1)}) custom-call(s32[16]{0:T(128)S(1)} %copy-done.2, s32[2,16]{1,0:T(2,128)S(1)} %copy-done.1, bf16[32,128,128]{2,1,0:T(8,128)(2,1)S(1)} %all-to-all-done.own_ref, bf16[4,64,128]{2,1,0:T(8,128)(2,1)S(1)} %get-tuple-element.19.keep_ref, ...), custom_call_target="tpu_custom_call" | custom-call | flops 536870912 | bytes 2097152 | tf_op jit(solution)/shard_map/attend_early/pallas_call | solution.py:370
  55.7 1.5 %all-to-all-done.1.query_ref = bf16[8,4,64,128]{3,2,1,0:T(8,128)(2,1)S(1)} async-done(((bf16[8,4,64,128]{3,2,1,0:T(8,128)(2,1)}), bf16[8,4,64,128]{3,2,1,0:T(8,128)(2,1)S(1)}, u32[]{:S(2)}, u32[]{:S(2)}) %all-to-all-start.1) | async-done | bytes 524320 | tf_op jit(solution)/shard_map/all_to_all | solution.py:173
  57.3 0.0 collective-permute-done.4.refs_2_
  57.3 0.0 collective-permute-done.5.refs_3_
  57.3 5.4 %attend_late.1 = bf16[32,64,128]{2,1,0:T(8,128)(2,1)S(1)} custom-call(s32[16]{0:T(128)S(1)} %copy-done.2, s32[2,16]{1,0:T(2,128)S(1)} %copy-done.1, bf16[32,128,128]{2,1,0:T(8,128)(2,1)S(1)} %all-to-all-done.own_ref, bf16[8,4,64,128]{3,2,1,0:T(8,128)(2,1)S(1)} %all-to-all-done.1.query_ref, bf16[4,64,128]{2,1,0:T(8,128)(2,1)S(1)} %get-tuple-element.19.keep_ref, ...), custom_call_target="tpu_custom_call" | custom-call | flops 2013265920 | bytes 2097152 | tf_op jit(solution)/shard_map/attend_late/pallas_call | solution.py:387
  62.7 22.6 %all_to_all.15.source = bf16[32,64,128]{2,1,0:T(8,128)(2,1)S(1)} all-to-all(bf16[32,64,128]{2,1,0:T(8,128)(2,1)S(1)} %attend_late.1), channel_id=1, replica_groups=mesh['shot'=16,'head'=32] {'head'}, dimensions={0} | all-to-all | bytes 1048576 | tf_op jit(solution)/shard_map/all_to_all | solution.py:399
  85.3 0.9 %join_heads.1 = bf16[64,4096]{1,0:T(8,128)(2,1)} custom-call(bf16[32,64,128]{2,1,0:T(8,128)(2,1)S(1)} %all_to_all.15.source), custom_call_target="tpu_custom_call" | custom-call | tf_op jit(solution)/shard_map/join_heads/pallas_call | solution.py:192
  (2 shorter events, 0.0 us)
Async XLA Ops:
  2.2 10.6 %copy-start = (bf16[1,64,4096]{2,1,0:T(8,128)(2,1)S(1)}, bf16[1,64,4096]{2,1,0:T(8,128)(2,1)}, u32[]{:S(2)}) copy-start(bf16[1,64,4096]{2,1,0:T(8,128)(2,1)} %param.6) | copy-start | bytes 1572868
  2.2 37.3 %all-to-all-start = ((bf16[32,128,128]{2,1,0:T(8,128)(2,1)}), bf16[32,128,128]{2,1,0:T(8,128)(2,1)S(1)}, u32[]{:S(2)}, u32[]{:S(2)}) async-start(bf16[32,128,128]{2,1,0:T(8,128)(2,1)} %split_heads.1), calls=%async_computation | async-start | bytes 2097152 | tf_op jit(solution)/shard_map/all_to_all | solution.py:399
  13.1 12.3 %collective-permute-start = (bf16[8,64,128]{2,1,0:T(8,128)(2,1)S(1)}, bf16[8,64,128]{2,1,0:T(8,128)(2,1)S(1)}, u32[]{:S(2)}, u32[]{:S(2)}) collective-permute-start(bf16[8,64,128]{2,1,0:T(8,128)(2,1)S(1)} %get-tuple-element.16), channel_id=1, source_target_pairs={{0,2},{1,3},{2,0},{3,1},{4,6},{5,7},{6,4},{7,5},{8,10},{9,11},{10,... | collective-permute-start | bytes 393224 | tf_op jit(solution)/shard_map/ppermute | solution.py:165
  16.4 15.0 %collective-permute-start.1 = (bf16[8,64,128]{2,1,0:T(8,128)(2,1)S(1)}, bf16[8,64,128]{2,1,0:T(8,128)(2,1)S(1)}, u32[]{:S(2)}, u32[]{:S(2)}) collective-permute-start(bf16[8,64,128]{2,1,0:T(8,128)(2,1)S(1)} %get-tuple-element.17), channel_id=1, source_target_pairs={{0,4},{1,5},{2,6},{3,7},{4,0},{5,1},{6,2},{7,3},{8,12},{9,13},{10,... | collective-permute-start | bytes 393224 | tf_op jit(solution)/shard_map/ppermute | solution.py:165
  20.7 13.2 %collective-permute-start.2 = (bf16[8,64,128]{2,1,0:T(8,128)(2,1)S(1)}, bf16[8,64,128]{2,1,0:T(8,128)(2,1)S(1)}, u32[]{:S(2)}, u32[]{:S(2)}) collective-permute-start(bf16[8,64,128]{2,1,0:T(8,128)(2,1)S(1)} %get-tuple-element.18), channel_id=1, source_target_pairs={{0,6},{1,7},{2,4},{3,5},{4,2},{5,3},{6,0},{7,1},{8,14},{9,15},{10,... | collective-permute-start | bytes 393224 | tf_op jit(solution)/shard_map/ppermute | solution.py:165
  34.8 8.2 %copy-start.3 = (s32[2,16,2]{1,2,0:T(2,128)S(1)}, s32[2,16,2]{1,2,0:T(2,128)}, u32[]{:S(2)}) copy-start(s32[2,16,2]{1,2,0:T(2,128)} %param.11) | copy-start | bytes 772
  39.5 17.8 %all-to-all-start.1 = ((bf16[8,4,64,128]{3,2,1,0:T(8,128)(2,1)}), bf16[8,4,64,128]{3,2,1,0:T(8,128)(2,1)S(1)}, u32[]{:S(2)}, u32[]{:S(2)}) async-start(bf16[8,4,64,128]{3,2,1,0:T(8,128)(2,1)} %pack_chips.1), calls=%async_computation.1 | async-start | bytes 1048576 | tf_op jit(solution)/shard_map/all_to_all | solution.py:173
  43.9 13.4 %collective-permute-start.4 = (bf16[4,128,128]{2,1,0:T(8,128)(2,1)S(1)}, bf16[4,128,128]{2,1,0:T(8,128)(2,1)S(1)}, u32[]{:S(2)}, u32[]{:S(2)}) collective-permute-start(bf16[4,128,128]{2,1,0:T(8,128)(2,1)S(1)} %get-tuple-element.23), channel_id=1, source_target_pairs={{0,256},{32,288},{64,320},{96,352},{128,384},{160,416},{192,448},{... | collective-permute-start | bytes 393224 | tf_op jit(solution)/shard_map/ppermute | solution.py:404
  48.1 9.1 %collective-permute-start.5 = (bf16[4,128,128]{2,1,0:T(8,128)(2,1)S(1)}, bf16[4,128,128]{2,1,0:T(8,128)(2,1)S(1)}, u32[]{:S(2)}, u32[]{:S(2)}) collective-permute-start(bf16[4,128,128]{2,1,0:T(8,128)(2,1)S(1)} %get-tuple-element.24), channel_id=1, source_target_pairs={{0,128},{32,160},{64,192},{96,224},{128,0},{160,32},{192,64},{224,... | collective-permute-start | bytes 393224 | tf_op jit(solution)/shard_map/ppermute | solution.py:404
  50.4 3.3 %copy-start.1 = (s32[2,16]{1,0:T(2,128)S(1)}, s32[2,16]{1,0:T(2,128)}, u32[]{:S(2)}) copy-start(s32[2,16]{1,0:T(2,128)} %links.3) | copy-start | bytes 388
  50.4 3.3 %copy-start.2 = (s32[16]{0:T(128)S(1)}, s32[16]{0:T(128)}, u32[]{:S(2)}) copy-start(s32[16]{0:T(128)} %lengths.3) | copy-start | bytes 196
  50.4 3.3 %collective-permute-start.3 = (bf16[4,64,128]{2,1,0:T(8,128)(2,1)S(1)}, bf16[4,64,128]{2,1,0:T(8,128)(2,1)S(1)}, u32[]{:S(2)}, u32[]{:S(2)}) collective-permute-start(bf16[4,64,128]{2,1,0:T(8,128)(2,1)S(1)} %get-tuple-element.20), channel_id=1, source_target_pairs={{0,1},{1,0},{2,3},{3,2},{4,5},{5,4},{6,7},{7,6},{8,9},{9,8},{10,11... | collective-permute-start | bytes 196616 | tf_op jit(solution)/shard_map/ppermute | solution.py:165

commit v6 on v5

--- a/solution.py
+++ b/solution.py
@@ -354,7 +354,7 @@
         finish_early,
     )
     chips = [(rz, core) for rz in range(1, 4) for core in range(2)]
-    attend_items([early, late_item(chips[:3]), late_item(chips[3:])], piece, own_ref)
+    attend_items([late_item(chips[:3]), late_item(chips[3:]), early], piece, own_ref)
 
 
 def attend_cost(queries, keys):

time: 86.8 us -> 86.8 us (level)
  no operation moved by 1% of the time
where the time goes in v6:
time: 86.8 us; the launch traced here: 86.2 us
  starting transfers between devices  32.6 us (38%)
  blocking collectives  22.6 us (26%)
  waiting for transfers between devices  18.4 us (21%)
  Pallas kernels  12.4 us (14%)
    all_to_all x1, blocking collectives, swap(): lax.all_to_all(array, 'head', split_axis=0, concat_axis=0, tiled=True)  22.6 us
    ppermute x4, waiting for transfers between devices, from_head(): lax.ppermute(array, 'head', [(low, low ^ flip) for low in range(count)])  12.1 us
    ppermute x4, starting transfers between devices, from_head(): lax.ppermute(array, 'head', [(low, low ^ flip) for low in range(count)])  12 us
    all_to_all x1, starting transfers between devices, swap(): lax.all_to_all(array, 'head', split_axis=0, concat_axis=0, tiled=True)  10.6 us
    ppermute x2, starting transfers between devices, from_partner(): lax.ppermute(array, 'shot', [(low, low ^ bit) for low in range(count)])  6.49 us
    pallas_call x1, Pallas kernels, attend_late(): pl.pallas_call(attend_late_kernel, in_specs=[smem, smem] + [vmem] * (6 +...  5.41 us
    all_to_all x1, waiting for transfers between devices, swap(): lax.all_to_all(array, 'head', split_axis=0, concat_axis=0, tiled=True)  4.7 us
    all_to_all x1, starting transfers between devices, gather_queries(): lax.all_to_all(pack_chips(by_y), 'head', split_axis=0, concat_axis=0, til...  3.45 us
  transfers between devices with their start and end apart: 8, of which 6 were waited for; matrix products, arithmetic and copies ran while one was open for 0% of the time, Pallas kernels for 5%

profile of v6, /device:TPU:1, one launch (start us, length us, event | category | flops | bytes accessed | tf_op | source)
XLA Modules:
  0.0 86.2 jit_solution(8882922067316334211)
XLA Ops:
  0.0 2.1 %split_heads.1 = bf16[32,128,128]{2,1,0:T(8,128)(2,1)} custom-call(bf16[64,4096]{1,0:T(8,128)(2,1)} %bitcast.5, bf16[64,4096]{1,0:T(8,128)(2,1)} %bitcast.6), custom_call_target="tpu_custom_call" | custom-call | tf_op jit(solution)/shard_map/split_heads/pallas_call | solution.py:69
  2.2 0.0 copy-start
  2.2 10.6 %all-to-all-start = ((bf16[32,128,128]{2,1,0:T(8,128)(2,1)}), bf16[32,128,128]{2,1,0:T(8,128)(2,1)S(1)}, u32[]{:S(2)}, u32[]{:S(2)}) async-start(bf16[32,128,128]{2,1,0:T(8,128)(2,1)} %split_heads.1), calls=%async_computation | async-start | bytes 2097152 | tf_op jit(solution)/shard_map/all_to_all | solution.py:399
  12.8 0.0 copy-done
  12.8 0.3 split_queries.1
  13.1 3.3 %collective-permute-start = (bf16[8,64,128]{2,1,0:T(8,128)(2,1)S(1)}, bf16[8,64,128]{2,1,0:T(8,128)(2,1)S(1)}, u32[]{:S(2)}, u32[]{:S(2)}) collective-permute-start(bf16[8,64,128]{2,1,0:T(8,128)(2,1)S(1)} %get-tuple-element.16), channel_id=1, source_target_pairs={{0,2},{1,3},{2,0},{3,1},{4,6},{5,7},{6,4},{7,5},{8,10},{9,11},{10,... | collective-permute-start | bytes 393224 | tf_op jit(solution)/shard_map/ppermute | solution.py:165
  16.4 4.3 %collective-permute-start.1 = (bf16[8,64,128]{2,1,0:T(8,128)(2,1)S(1)}, bf16[8,64,128]{2,1,0:T(8,128)(2,1)S(1)}, u32[]{:S(2)}, u32[]{:S(2)}) collective-permute-start(bf16[8,64,128]{2,1,0:T(8,128)(2,1)S(1)} %get-tuple-element.17), channel_id=1, source_target_pairs={{0,4},{1,5},{2,6},{3,7},{4,0},{5,1},{6,2},{7,3},{8,12},{9,13},{10,... | collective-permute-start | bytes 393224 | tf_op jit(solution)/shard_map/ppermute | solution.py:165
  20.7 2.0 %collective-permute-start.2 = (bf16[8,64,128]{2,1,0:T(8,128)(2,1)S(1)}, bf16[8,64,128]{2,1,0:T(8,128)(2,1)S(1)}, u32[]{:S(2)}, u32[]{:S(2)}) collective-permute-start(bf16[8,64,128]{2,1,0:T(8,128)(2,1)S(1)} %get-tuple-element.18), channel_id=1, source_target_pairs={{0,6},{1,7},{2,4},{3,5},{4,2},{5,3},{6,0},{7,1},{8,14},{9,15},{10,... | collective-permute-start | bytes 393224 | tf_op jit(solution)/shard_map/ppermute | solution.py:165
  22.7 2.7 %collective-permute-done.refs_1_ = bf16[8,64,128]{2,1,0:T(8,128)(2,1)S(1)} collective-permute-done((bf16[8,64,128]{2,1,0:T(8,128)(2,1)S(1)}, bf16[8,64,128]{2,1,0:T(8,128)(2,1)S(1)}, u32[]{:S(2)}, u32[]{:S(2)}) %collective-permute-start) | collective-permute-done | bytes 131104 | tf_op jit(solution)/shard_map/ppermute | solution.py:165
  25.4 5.9 %collective-permute-done.1.refs_2_ = bf16[8,64,128]{2,1,0:T(8,128)(2,1)S(1)} collective-permute-done((bf16[8,64,128]{2,1,0:T(8,128)(2,1)S(1)}, bf16[8,64,128]{2,1,0:T(8,128)(2,1)S(1)}, u32[]{:S(2)}, u32[]{:S(2)}) %collective-permute-start.1) | collective-permute-done | bytes 131104 | tf_op jit(solution)/shard_map/ppermute | solution.py:165
  31.3 2.6 %collective-permute-done.2.refs_3_ = bf16[8,64,128]{2,1,0:T(8,128)(2,1)S(1)} collective-permute-done((bf16[8,64,128]{2,1,0:T(8,128)(2,1)S(1)}, bf16[8,64,128]{2,1,0:T(8,128)(2,1)S(1)}, u32[]{:S(2)}, u32[]{:S(2)}) %collective-permute-start.2) | collective-permute-done | bytes 131104 | tf_op jit(solution)/shard_map/ppermute | solution.py:165
  33.9 0.8 pack_chips.1
  34.8 4.7 %all-to-all-done.own_ref = bf16[32,128,128]{2,1,0:T(8,128)(2,1)S(1)} async-done(((bf16[32,128,128]{2,1,0:T(8,128)(2,1)}), bf16[32,128,128]{2,1,0:T(8,128)(2,1)S(1)}, u32[]{:S(2)}, u32[]{:S(2)}) %all-to-all-start) | async-done | bytes 1048608 | tf_op jit(solution)/shard_map/all_to_all | solution.py:399
  39.5 3.4 %all-to-all-start.1 = ((bf16[8,4,64,128]{3,2,1,0:T(8,128)(2,1)}), bf16[8,4,64,128]{3,2,1,0:T(8,128)(2,1)S(1)}, u32[]{:S(2)}, u32[]{:S(2)}) async-start(bf16[8,4,64,128]{3,2,1,0:T(8,128)(2,1)} %pack_chips.1), calls=%async_computation.1 | async-start | bytes 1048576 | tf_op jit(solution)/shard_map/all_to_all | solution.py:173
  42.9 0.0 copy-done.3
  42.9 0.1 copy.7.block_select
  43.0 0.8 pick_blocks.1
  43.9 4.3 %collective-permute-start.4 = (bf16[4,128,128]{2,1,0:T(8,128)(2,1)S(1)}, bf16[4,128,128]{2,1,0:T(8,128)(2,1)S(1)}, u32[]{:S(2)}, u32[]{:S(2)}) collective-permute-start(bf16[4,128,128]{2,1,0:T(8,128)(2,1)S(1)} %get-tuple-element.23), channel_id=1, source_target_pairs={{0,256},{32,288},{64,320},{96,352},{128,384},{160,416},{192,448},{... | collective-permute-start | bytes 393224 | tf_op jit(solution)/shard_map/ppermute | solution.py:404
  48.1 2.2 %collective-permute-start.5 = (bf16[4,128,128]{2,1,0:T(8,128)(2,1)S(1)}, bf16[4,128,128]{2,1,0:T(8,128)(2,1)S(1)}, u32[]{:S(2)}, u32[]{:S(2)}) collective-permute-start(bf16[4,128,128]{2,1,0:T(8,128)(2,1)S(1)} %get-tuple-element.24), channel_id=1, source_target_pairs={{0,128},{32,160},{64,192},{96,224},{128,0},{160,32},{192,64},{224,... | collective-permute-start | bytes 393224 | tf_op jit(solution)/shard_map/ppermute | solution.py:404
  50.4 0.0 copy-start.1
  50.4 0.0 copy-start.2
  50.4 2.4 %collective-permute-start.3 = (bf16[4,64,128]{2,1,0:T(8,128)(2,1)S(1)}, bf16[4,64,128]{2,1,0:T(8,128)(2,1)S(1)}, u32[]{:S(2)}, u32[]{:S(2)}) collective-permute-start(bf16[4,64,128]{2,1,0:T(8,128)(2,1)S(1)} %get-tuple-element.20), channel_id=1, source_target_pairs={{0,1},{1,0},{2,3},{3,2},{4,5},{5,4},{6,7},{7,6},{8,9},{9,8},{10,11... | collective-permute-start | bytes 196616 | tf_op jit(solution)/shard_map/ppermute | solution.py:165
  52.9 0.9 %collective-permute-done.3.come_ref = bf16[4,64,128]{2,1,0:T(8,128)(2,1)S(1)} collective-permute-done((bf16[4,64,128]{2,1,0:T(8,128)(2,1)S(1)}, bf16[4,64,128]{2,1,0:T(8,128)(2,1)S(1)}, u32[]{:S(2)}, u32[]{:S(2)}) %collective-permute-start.3) | collective-permute-done | bytes 65568 | tf_op jit(solution)/shard_map/ppermute | solution.py:165
  53.7 0.0 copy-done.1
  53.7 0.0 copy-done.2
  53.7 2.0 %attend_early.1 = (f32[512,256]{1,0:T(8,128)S(1)}, f32[512,128]{1,0:T(8,128)S(1)}) custom-call(s32[16]{0:T(128)S(1)} %copy-done.2, s32[2,16]{1,0:T(2,128)S(1)} %copy-done.1, bf16[32,128,128]{2,1,0:T(8,128)(2,1)S(1)} %all-to-all-done.own_ref, bf16[4,64,128]{2,1,0:T(8,128)(2,1)S(1)} %get-tuple-element.19.keep_ref, ...), custom_call_target="tpu_custom_call" | custom-call | flops 536870912 | bytes 2097152 | tf_op jit(solution)/shard_map/attend_early/pallas_call | solution.py:370
  55.7 1.5 %all-to-all-done.1.query_ref = bf16[8,4,64,128]{3,2,1,0:T(8,128)(2,1)S(1)} async-done(((bf16[8,4,64,128]{3,2,1,0:T(8,128)(2,1)}), bf16[8,4,64,128]{3,2,1,0:T(8,128)(2,1)S(1)}, u32[]{:S(2)}, u32[]{:S(2)}) %all-to-all-start.1) | async-done | bytes 524320 | tf_op jit(solution)/shard_map/all_to_all | solution.py:173
  57.3 0.0 collective-permute-done.4.refs_2_
  57.3 0.0 collective-permute-done.5.refs_3_
  57.3 5.4 %attend_late.1 = bf16[32,64,128]{2,1,0:T(8,128)(2,1)S(1)} custom-call(s32[16]{0:T(128)S(1)} %copy-done.2, s32[2,16]{1,0:T(2,128)S(1)} %copy-done.1, bf16[32,128,128]{2,1,0:T(8,128)(2,1)S(1)} %all-to-all-done.own_ref, bf16[8,4,64,128]{3,2,1,0:T(8,128)(2,1)S(1)} %all-to-all-done.1.query_ref, bf16[4,64,128]{2,1,0:T(8,128)(2,1)S(1)} %get-tuple-element.19.keep_ref, ...), custom_call_target="tpu_custom_call" | custom-call | flops 2013265920 | bytes 2097152 | tf_op jit(solution)/shard_map/attend_late/pallas_call | solution.py:387
  62.7 22.6 %all_to_all.15.source = bf16[32,64,128]{2,1,0:T(8,128)(2,1)S(1)} all-to-all(bf16[32,64,128]{2,1,0:T(8,128)(2,1)S(1)} %attend_late.1), channel_id=1, replica_groups=mesh['shot'=16,'head'=32] {'head'}, dimensions={0} | all-to-all | bytes 1048576 | tf_op jit(solution)/shard_map/all_to_all | solution.py:399
  85.4 0.9 %join_heads.1 = bf16[64,4096]{1,0:T(8,128)(2,1)} custom-call(bf16[32,64,128]{2,1,0:T(8,128)(2,1)S(1)} %all_to_all.15.source), custom_call_target="tpu_custom_call" | custom-call | tf_op jit(solution)/shard_map/join_heads/pallas_call | solution.py:192
  (2 shorter events, 0.0 us)
Async XLA Ops:
  2.2 10.6 %copy-start = (bf16[1,64,4096]{2,1,0:T(8,128)(2,1)S(1)}, bf16[1,64,4096]{2,1,0:T(8,128)(2,1)}, u32[]{:S(2)}) copy-start(bf16[1,64,4096]{2,1,0:T(8,128)(2,1)} %param.6) | copy-start | bytes 1572868
  2.2 37.3 %all-to-all-start = ((bf16[32,128,128]{2,1,0:T(8,128)(2,1)}), bf16[32,128,128]{2,1,0:T(8,128)(2,1)S(1)}, u32[]{:S(2)}, u32[]{:S(2)}) async-start(bf16[32,128,128]{2,1,0:T(8,128)(2,1)} %split_heads.1), calls=%async_computation | async-start | bytes 2097152 | tf_op jit(solution)/shard_map/all_to_all | solution.py:399
  13.1 12.3 %collective-permute-start = (bf16[8,64,128]{2,1,0:T(8,128)(2,1)S(1)}, bf16[8,64,128]{2,1,0:T(8,128)(2,1)S(1)}, u32[]{:S(2)}, u32[]{:S(2)}) collective-permute-start(bf16[8,64,128]{2,1,0:T(8,128)(2,1)S(1)} %get-tuple-element.16), channel_id=1, source_target_pairs={{0,2},{1,3},{2,0},{3,1},{4,6},{5,7},{6,4},{7,5},{8,10},{9,11},{10,... | collective-permute-start | bytes 393224 | tf_op jit(solution)/shard_map/ppermute | solution.py:165
  16.4 15.0 %collective-permute-start.1 = (bf16[8,64,128]{2,1,0:T(8,128)(2,1)S(1)}, bf16[8,64,128]{2,1,0:T(8,128)(2,1)S(1)}, u32[]{:S(2)}, u32[]{:S(2)}) collective-permute-start(bf16[8,64,128]{2,1,0:T(8,128)(2,1)S(1)} %get-tuple-element.17), channel_id=1, source_target_pairs={{0,4},{1,5},{2,6},{3,7},{4,0},{5,1},{6,2},{7,3},{8,12},{9,13},{10,... | collective-permute-start | bytes 393224 | tf_op jit(solution)/shard_map/ppermute | solution.py:165
  20.7 13.2 %collective-permute-start.2 = (bf16[8,64,128]{2,1,0:T(8,128)(2,1)S(1)}, bf16[8,64,128]{2,1,0:T(8,128)(2,1)S(1)}, u32[]{:S(2)}, u32[]{:S(2)}) collective-permute-start(bf16[8,64,128]{2,1,0:T(8,128)(2,1)S(1)} %get-tuple-element.18), channel_id=1, source_target_pairs={{0,6},{1,7},{2,4},{3,5},{4,2},{5,3},{6,0},{7,1},{8,14},{9,15},{10,... | collective-permute-start | bytes 393224 | tf_op jit(solution)/shard_map/ppermute | solution.py:165
  34.8 8.2 %copy-start.3 = (s32[2,16,2]{1,2,0:T(2,128)S(1)}, s32[2,16,2]{1,2,0:T(2,128)}, u32[]{:S(2)}) copy-start(s32[2,16,2]{1,2,0:T(2,128)} %param.11) | copy-start | bytes 772
  39.5 17.8 %all-to-all-start.1 = ((bf16[8,4,64,128]{3,2,1,0:T(8,128)(2,1)}), bf16[8,4,64,128]{3,2,1,0:T(8,128)(2,1)S(1)}, u32[]{:S(2)}, u32[]{:S(2)}) async-start(bf16[8,4,64,128]{3,2,1,0:T(8,128)(2,1)} %pack_chips.1), calls=%async_computation.1 | async-start | bytes 1048576 | tf_op jit(solution)/shard_map/all_to_all | solution.py:173
  43.9 13.4 %collective-permute-start.4 = (bf16[4,128,128]{2,1,0:T(8,128)(2,1)S(1)}, bf16[4,128,128]{2,1,0:T(8,128)(2,1)S(1)}, u32[]{:S(2)}, u32[]{:S(2)}) collective-permute-start(bf16[4,128,128]{2,1,0:T(8,128)(2,1)S(1)} %get-tuple-element.23), channel_id=1, source_target_pairs={{0,256},{32,288},{64,320},{96,352},{128,384},{160,416},{192,448},{... | collective-permute-start | bytes 393224 | tf_op jit(solution)/shard_map/ppermute | solution.py:404
  48.1 9.1 %collective-permute-start.5 = (bf16[4,128,128]{2,1,0:T(8,128)(2,1)S(1)}, bf16[4,128,128]{2,1,0:T(8,128)(2,1)S(1)}, u32[]{:S(2)}, u32[]{:S(2)}) collective-permute-start(bf16[4,128,128]{2,1,0:T(8,128)(2,1)S(1)} %get-tuple-element.24), channel_id=1, source_target_pairs={{0,128},{32,160},{64,192},{96,224},{128,0},{160,32},{192,64},{224,... | collective-permute-start | bytes 393224 | tf_op jit(solution)/shard_map/ppermute | solution.py:404
  50.4 3.3 %copy-start.1 = (s32[2,16]{1,0:T(2,128)S(1)}, s32[2,16]{1,0:T(2,128)}, u32[]{:S(2)}) copy-start(s32[2,16]{1,0:T(2,128)} %links.3) | copy-start | bytes 388
  50.4 3.3 %copy-start.2 = (s32[16]{0:T(128)S(1)}, s32[16]{0:T(128)}, u32[]{:S(2)}) copy-start(s32[16]{0:T(128)} %lengths.3) | copy-start | bytes 196
  50.4 3.3 %collective-permute-start.3 = (bf16[4,64,128]{2,1,0:T(8,128)(2,1)S(1)}, bf16[4,64,128]{2,1,0:T(8,128)(2,1)S(1)}, u32[]{:S(2)}, u32[]{:S(2)}) collective-permute-start(bf16[4,64,128]{2,1,0:T(8,128)(2,1)S(1)} %get-tuple-element.20), channel_id=1, source_target_pairs={{0,1},{1,0},{2,3},{3,2},{4,5},{5,4},{6,7},{7,6},{8,9},{9,8},{10,11... | collective-permute-start | bytes 196616 | tf_op jit(solution)/shard_map/ppermute | solution.py:165
